TPU v7x, 32 devices: a whole 2x2x4 slice. The times are simulated.
32 devices in a mesh: dp: 4 (over x, core), fsdp: 8 (over z, y).
Axes of the slice: x: 2, y: 2, z: 4, core: 2. Of those that a mesh axis runs over, the one named last changes fastest.
Arguments:
- tokens: bfloat16 [4096, 2048], P(('dp', 'fsdp')), may hold values from -6 to 6
- triple_weight: bfloat16 [2048, 6144], P(('dp', 'fsdp')), may hold values from -0.125 to 0.125
- output_weight: bfloat16 [2048, 2048], P(('dp', 'fsdp')), may hold values from -1 to 1
- up_weight: bfloat16 [2048, 8192], P(('dp', 'fsdp')), may hold values from -0.125 to 0.125
- down_weight: bfloat16 [8192, 2048], P(('dp', 'fsdp')), may hold values from -0.0625 to 0.0625
- first_gain: bfloat16 [2048], P(('dp', 'fsdp')), may hold values from 0.5 to 1.5
- second_gain: bfloat16 [2048], P(('dp', 'fsdp')), may hold values from 0.5 to 1.5
- cotangent: bfloat16 [4096, 2048], P(('dp', 'fsdp')), may hold values from -6 to 6
- frame_counts: int32 [4, 2], P('dp'), may hold values from 1 to 4
- text_counts: int32 [4, 2, 4], P('dp'), may hold values from 0 to 32
- action_counts: int32 [4, 2, 4], P('dp'), may hold values from 0 to 2
Outputs:
- layer_output: bfloat16 [4096, 2048], P(('dp', 'fsdp'))
- token_grad: bfloat16 [4096, 2048], P(('dp', 'fsdp'))
- triple_grad: float32 [2048, 6144], P(('dp', 'fsdp'))
- output_grad: float32 [2048, 2048], P(('dp', 'fsdp'))
- up_grad: float32 [2048, 8192], P(('dp', 'fsdp'))
- down_grad: float32 [8192, 2048], P(('dp', 'fsdp'))
- first_gain_grad: float32 [2048], P(('dp', 'fsdp'))
- second_gain_grad: float32 [2048], P(('dp', 'fsdp'))
All inputs are finite; a program needn't handle non-finite values.
Results may differ from a plain program's by a relative error of at most 0.015.
Values may be sent and summed in bfloat16 or wider, within the bound.
No kernel may reach another device: no remote copies, remote signals or barrier semaphores. Data moves between devices by JAX's collectives and lax.ppermute only.
A program may use at most 512 MiB of HBM per device.

v0:
```python
import math

import jax
import jax.numpy as jnp
from jax import lax
from jax.sharding import PartitionSpec as P

HEADS = 16
HEAD = 128
IMG = 576


EPSILON = 1e-05
MASKED = -1e30


def clip_layout(frame_counts, text_counts, action_counts, pack_length):
    frame_slot = jnp.arange(text_counts.shape[-1], dtype=jnp.int32)
    frame_live = frame_slot < frame_counts[..., None]
    frame_sizes = jnp.where(frame_live, IMG + text_counts + action_counts, 0)
    clip_lengths = jnp.sum(frame_sizes, axis=-1)
    first_end = clip_lengths[..., 0:1]
    second_end = first_end + clip_lengths[..., 1:2]
    places = jnp.arange(pack_length, dtype=jnp.int32)
    segment = (places >= first_end).astype(jnp.int32) + (places >= second_end).astype(jnp.int32)
    starts = jnp.where(segment == 0, 0, jnp.where(segment == 1, first_end, second_end))
    return (segment, places - starts)


def rotary_tables(position):
    half_width = HEAD // 2
    frequency = jnp.exp(
        jnp.arange(half_width, dtype=jnp.float32) * (-2.0 * math.log(10000.0) / HEAD)
    )
    angles = position.astype(jnp.float32)[:, None] * frequency[None, :]
    return (jnp.cos(angles)[:, None, :], jnp.sin(angles)[:, None, :])


def rotate(vectors, cosine, sine_table):
    half_width = vectors.shape[-1] // 2
    former = vectors[..., :half_width]
    latter = vectors[..., half_width:]
    return jnp.concatenate(
        [former * cosine - latter * sine_table, latter * cosine + former * sine_table], axis=-1
    )


def unrotate(gradient, cosine, sine_table):
    half_width = gradient.shape[-1] // 2
    former = gradient[..., :half_width]
    latter = gradient[..., half_width:]
    return jnp.concatenate(
        [former * cosine + latter * sine_table, latter * cosine - former * sine_table], axis=-1
    )


def norm_rows(values, gain_vector):
    centred = values - jnp.mean(values, axis=-1, keepdims=True)
    variance = jnp.mean(centred * centred, axis=-1, keepdims=True)
    return centred * lax.rsqrt(variance + EPSILON) * gain_vector


def block_allowed(query_segment, query_places, key_segment, key_place):
    return (query_segment[:, None] == key_segment[None, :]) & (
        key_place[None, :] <= query_places[:, None]
    )


def block_scores(queries, key_block, allowed):
    scores = jnp.einsum(
        "qhd,khd->hqk", queries, key_block, preferred_element_type=jnp.float32
    ) * HEAD ** (-0.5)
    return jnp.where(allowed[None], scores, MASKED)


def block_probs(queries, key_block, allowed, row_max, row_sum):
    scores = block_scores(queries, key_block, allowed)
    return jnp.where(allowed[None], jnp.exp(scores - row_max[..., None]) / row_sum[..., None], 0.0)


def softmax_stats(queries, key_blocks, layout_parts):
    query_segment, query_places, key_segments, key_places = layout_parts
    row_count, head_count = (queries.shape[0], queries.shape[1])
    start_state = (
        jnp.full((head_count, row_count), MASKED, jnp.float32),
        jnp.zeros((head_count, row_count), jnp.float32),
    )

    def advance(state, block_inputs):
        key_block, key_segment, key_place = block_inputs
        allowed = block_allowed(query_segment, query_places, key_segment, key_place)

        def update(current):
            row_max, row_sum = current
            scores = block_scores(queries, key_block, allowed)
            new_max = jnp.maximum(row_max, jnp.max(scores, axis=-1))
            weights = jnp.where(allowed[None], jnp.exp(scores - new_max[..., None]), 0.0)
            return (new_max, row_sum * jnp.exp(row_max - new_max) + jnp.sum(weights, axis=-1))

        return (lax.cond(jnp.any(allowed), update, lambda current: current, state), None)

    final_state, unused = lax.scan(advance, start_state, (key_blocks, key_segments, key_places))
    return final_state


def attention_output(queries, key_blocks, value_blocks, layout_parts, row_max, row_sum):
    query_segment, query_places, key_segments, key_places = layout_parts

    def advance(accum, block_inputs):
        key_block, value_block, key_segment, key_place = block_inputs
        allowed = block_allowed(query_segment, query_places, key_segment, key_place)

        def update(current):
            probs = block_probs(queries, key_block, allowed, row_max, row_sum).astype(jnp.bfloat16)
            return current + jnp.einsum(
                "hqk,khd->qhd", probs, value_block, preferred_element_type=jnp.float32
            )

        return (lax.cond(jnp.any(allowed), update, lambda current: current, accum), None)

    attended, unused = lax.scan(
        advance,
        jnp.zeros(queries.shape, jnp.float32),
        (key_blocks, value_blocks, key_segments, key_places),
    )
    return attended


def attention_backward(
    queries, grad_attended, delta_rows, key_blocks, value_blocks, layout_parts, row_max, row_sum
):
    query_segment, query_places, key_segments, key_places = layout_parts
    score_scale = HEAD ** (-0.5)

    def advance(grad_query, block_inputs):
        key_block, value_block, key_segment, key_place = block_inputs
        allowed = block_allowed(query_segment, query_places, key_segment, key_place)

        def update(current):
            probs = block_probs(queries, key_block, allowed, row_max, row_sum)
            grad_probs = jnp.einsum(
                "qhd,khd->hqk", grad_attended, value_block, preferred_element_type=jnp.float32
            )
            grad_scores = (probs * (grad_probs - delta_rows[..., None])).astype(jnp.bfloat16)
            new_query = (
                current
                + jnp.einsum(
                    "hqk,khd->qhd", grad_scores, key_block, preferred_element_type=jnp.float32
                )
                * score_scale
            )
            return (new_query, ())

        def bypass(current):
            return (current, ())

        return lax.cond(jnp.any(allowed), update, bypass, grad_query)

    grad_query, terms = lax.scan(
        advance,
        jnp.zeros(queries.shape, jnp.float32),
        (key_blocks, value_blocks, key_segments, key_places),
    )
    return (grad_query, None, None)


def project_front(inputs, triple_full, gain_full, cosine, sine_table):
    row_count, width = inputs.shape
    normed = norm_rows(inputs, gain_full.astype(jnp.float32)).astype(jnp.bfloat16)
    mixed = jnp.dot(normed, triple_full, preferred_element_type=jnp.float32)
    queries = rotate(mixed[:, :width].reshape(row_count, HEADS, HEAD), cosine, sine_table).astype(
        jnp.bfloat16
    )
    keys_local = (
        rotate(mixed[:, width : 2 * width].reshape(row_count, HEADS, HEAD), cosine, sine_table)
        .astype(jnp.bfloat16)
        .reshape(row_count, width)
    )
    values_local = mixed[:, 2 * width :].astype(jnp.bfloat16)
    return (normed, queries, keys_local, values_local)


def run_attention(queries, gathered, layout_parts):
    block_count = layout_parts[2].shape[0]
    key_blocks = gathered[0].reshape(block_count, -1, HEADS, HEAD)
    value_blocks = gathered[1].reshape(block_count, -1, HEADS, HEAD)
    row_max, row_sum = softmax_stats(queries, key_blocks, layout_parts)
    attended = attention_output(queries, key_blocks, value_blocks, layout_parts, row_max, row_sum)
    return (attended, key_blocks, value_blocks, row_max, row_sum)


def finish_layer(inputs, attended, output_full, up_full, down_full, second_full):
    row_count, width = inputs.shape
    attended_low = attended.reshape(row_count, width).astype(jnp.bfloat16)
    middle = inputs + jnp.dot(attended_low, output_full, preferred_element_type=jnp.float32)
    normed_two = norm_rows(middle, second_full.astype(jnp.float32)).astype(jnp.bfloat16)
    hidden = jnp.dot(normed_two, up_full, preferred_element_type=jnp.float32)
    activation = jax.nn.gelu(hidden).astype(jnp.bfloat16)
    result = middle + jnp.dot(activation, down_full, preferred_element_type=jnp.float32)
    return (result, attended_low, middle, normed_two, hidden, activation)


def body(
    tokens,
    triple_weight,
    output_weight,
    up_weight,
    down_weight,
    first_gain,
    second_gain,
    cotangent,
    frame_counts,
    text_counts,
    action_counts,
):
    row_count, width = tokens.shape
    pack_length = row_count * lax.axis_size("fsdp")
    first_place = lax.axis_index("fsdp") * row_count
    segment, position = clip_layout(frame_counts[0], text_counts[0], action_counts[0], pack_length)
    block_rows = min(1024, pack_length)
    block_count = pack_length // block_rows
    query_places = first_place + jnp.arange(row_count, dtype=jnp.int32)
    own_segment = lax.dynamic_slice_in_dim(segment, first_place, row_count, 0)
    layout_parts = (
        own_segment,
        query_places,
        segment.reshape(block_count, block_rows),
        jnp.arange(pack_length, dtype=jnp.int32).reshape(block_count, block_rows),
    )
    cosine, sine_table = rotary_tables(
        lax.dynamic_slice_in_dim(position, first_place, row_count, 0)
    )
    inputs = tokens.astype(jnp.float32)
    attention_set = (
        lax.all_gather(triple_weight, ("dp", "fsdp"), axis=0, tiled=True),
        lax.all_gather(output_weight, ("dp", "fsdp"), axis=0, tiled=True),
        lax.all_gather(first_gain, ("dp", "fsdp"), axis=0, tiled=True),
    )
    normed, queries, keys_local, values_local = project_front(
        inputs, attention_set[0], attention_set[2], cosine, sine_table
    )
    gathered = (
        lax.all_gather(keys_local, "fsdp", axis=0, tiled=True),
        lax.all_gather(values_local, "fsdp", axis=0, tiled=True),
    )
    attended, key_blocks, value_blocks, row_max, row_sum = run_attention(
        queries, gathered, layout_parts
    )
    feedforward_set = (
        lax.all_gather(up_weight, ("dp", "fsdp"), axis=0, tiled=True),
        lax.all_gather(down_weight, ("dp", "fsdp"), axis=0, tiled=True),
        lax.all_gather(second_gain, ("dp", "fsdp"), axis=0, tiled=True),
    )
    kept_parts = finish_layer(
        inputs,
        attended,
        attention_set[1],
        feedforward_set[0],
        feedforward_set[1],
        feedforward_set[2],
    )
    layer_output = kept_parts[0].astype(jnp.bfloat16)
    attention_set = (
        lax.all_gather(triple_weight, ("dp", "fsdp"), axis=0, tiled=True),
        lax.all_gather(output_weight, ("dp", "fsdp"), axis=0, tiled=True),
        lax.all_gather(first_gain, ("dp", "fsdp"), axis=0, tiled=True),
    )
    normed, queries, keys_local, values_local = project_front(
        inputs, attention_set[0], attention_set[2], cosine, sine_table
    )
    gathered = (
        lax.all_gather(keys_local, "fsdp", axis=0, tiled=True),
        lax.all_gather(values_local, "fsdp", axis=0, tiled=True),
    )
    attended, key_blocks, value_blocks, row_max, row_sum = run_attention(
        queries, gathered, layout_parts
    )
    feedforward_set = (
        lax.all_gather(up_weight, ("dp", "fsdp"), axis=0, tiled=True),
        lax.all_gather(down_weight, ("dp", "fsdp"), axis=0, tiled=True),
        lax.all_gather(second_gain, ("dp", "fsdp"), axis=0, tiled=True),
    )
    kept_parts = finish_layer(
        inputs,
        attended,
        attention_set[1],
        feedforward_set[0],
        feedforward_set[1],
        feedforward_set[2],
    )
    unused_result, attended_low, middle, normed_two, hidden, activation = kept_parts
    down_term = jnp.einsum("rf,rd->fd", activation, cotangent, preferred_element_type=jnp.float32)
    grad_activation = jnp.einsum(
        "rd,fd->rf", cotangent, feedforward_set[1], preferred_element_type=jnp.float32
    )
    unused_gelu, gelu_pull = jax.vjp(jax.nn.gelu, hidden)
    grad_hidden = gelu_pull(grad_activation)[0].astype(jnp.bfloat16)
    up_term = jnp.einsum("rd,rf->df", normed_two, grad_hidden, preferred_element_type=jnp.float32)
    grad_normed_two = jnp.einsum(
        "rf,df->rd", grad_hidden, feedforward_set[0], preferred_element_type=jnp.float32
    )
    unused_second, second_pull = jax.vjp(norm_rows, middle, feedforward_set[2].astype(jnp.float32))
    grad_middle_norm, second_gain_term = second_pull(grad_normed_two)
    grad_middle = cotangent.astype(jnp.float32) + grad_middle_norm
    feedforward_sums = (
        lax.psum_scatter(up_term, ("dp", "fsdp"), scatter_dimension=0, tiled=True),
        lax.psum_scatter(down_term, ("dp", "fsdp"), scatter_dimension=0, tiled=True),
        lax.psum_scatter(second_gain_term, ("dp", "fsdp"), scatter_dimension=0, tiled=True),
    )
    grad_branch = grad_middle.astype(jnp.bfloat16)
    output_term = jnp.einsum(
        "rd,re->de", attended_low, grad_branch, preferred_element_type=jnp.float32
    )
    grad_attended = (
        jnp.einsum("re,de->rd", grad_branch, attention_set[1], preferred_element_type=jnp.float32)
        .astype(jnp.bfloat16)
        .reshape(row_count, HEADS, HEAD)
    )
    delta_rows = jnp.sum(grad_attended.astype(jnp.float32) * attended, axis=-1).T
    score_scale = HEAD ** (-0.5)
    grad_query = attention_backward(
        queries, grad_attended, delta_rows, key_blocks, value_blocks, layout_parts, row_max, row_sum
    )[0]
    pack_stats = (
        lax.all_gather(row_max.T, "fsdp", axis=0, tiled=True),
        lax.all_gather(row_sum.T, "fsdp", axis=0, tiled=True),
        lax.all_gather(delta_rows.T, "fsdp", axis=0, tiled=True),
    )
    own_keys = keys_local.reshape(row_count, HEADS, HEAD)
    own_values = values_local.reshape(row_count, HEADS, HEAD)
    empty_grads = jnp.zeros((row_count, HEADS, HEAD), jnp.float32)
    query_piece = lax.all_gather(queries, "fsdp", axis=0, tiled=True)
    grad_piece = lax.all_gather(grad_attended, "fsdp", axis=0, tiled=True)
    piece_rows = query_piece.shape[0]
    block_size = min(1024, piece_rows)
    block_total = piece_rows // block_size

    def advance(current, block_index):
        offset = block_index * block_size
        query_part = lax.dynamic_slice_in_dim(query_piece, offset, block_size, 0)
        grad_part = lax.dynamic_slice_in_dim(grad_piece, offset, block_size, 0)
        max_part = lax.dynamic_slice_in_dim(pack_stats[0], offset, block_size, 0).T
        sum_part = lax.dynamic_slice_in_dim(pack_stats[1], offset, block_size, 0).T
        delta_part = lax.dynamic_slice_in_dim(pack_stats[2], offset, block_size, 0).T
        part_segment = lax.dynamic_slice_in_dim(segment, offset, block_size, 0)
        part_places = offset + jnp.arange(block_size, dtype=jnp.int32)
        allowed = block_allowed(part_segment, part_places, own_segment, query_places)

        def update(pair):
            probs = block_probs(query_part, own_keys, allowed, max_part, sum_part)
            grad_probs = jnp.einsum(
                "qhd,khd->hqk", grad_part, own_values, preferred_element_type=jnp.float32
            )
            grad_scores = (probs * (grad_probs - delta_part[..., None])).astype(jnp.bfloat16)
            grad_key = (
                pair[0]
                + jnp.einsum(
                    "hqk,qhd->khd", grad_scores, query_part, preferred_element_type=jnp.float32
                )
                * score_scale
            )
            grad_value = pair[1] + jnp.einsum(
                "hqk,qhd->khd",
                probs.astype(jnp.bfloat16),
                grad_part,
                preferred_element_type=jnp.float32,
            )
            return (grad_key, grad_value)

        return (lax.cond(jnp.any(allowed), update, lambda pair: pair, current), None)

    result, unused = lax.scan(
        advance, (empty_grads, empty_grads), jnp.arange(block_total, dtype=jnp.int32)
    )
    key_grad_sum = result[0].reshape(row_count, width)
    value_grad_sum = result[1].reshape(row_count, width)
    grad_query_full = (
        unrotate(grad_query, cosine, sine_table).reshape(row_count, width).astype(jnp.bfloat16)
    )
    grad_key_full = (
        unrotate(key_grad_sum.reshape(row_count, HEADS, HEAD), cosine, sine_table)
        .reshape(row_count, width)
        .astype(jnp.bfloat16)
    )
    grad_value_full = value_grad_sum.astype(jnp.bfloat16)
    grad_mixed = jnp.concatenate([grad_query_full, grad_key_full, grad_value_full], axis=1)
    triple_term = jnp.einsum("rd,re->de", normed, grad_mixed, preferred_element_type=jnp.float32)
    grad_normed = jnp.einsum(
        "re,de->rd", grad_mixed, attention_set[0], preferred_element_type=jnp.float32
    )
    unused_first, first_pull = jax.vjp(norm_rows, inputs, attention_set[2].astype(jnp.float32))
    grad_input_norm, first_gain_term = first_pull(grad_normed)
    token_grad = (grad_middle + grad_input_norm).astype(jnp.bfloat16)
    attention_sums = (
        lax.psum_scatter(triple_term, ("dp", "fsdp"), scatter_dimension=0, tiled=True),
        lax.psum_scatter(output_term, ("dp", "fsdp"), scatter_dimension=0, tiled=True),
        lax.psum_scatter(first_gain_term, ("dp", "fsdp"), scatter_dimension=0, tiled=True),
    )
    return (
        layer_output,
        token_grad,
        attention_sums[0],
        attention_sums[1],
        feedforward_sums[0],
        feedforward_sums[1],
        attention_sums[2],
        feedforward_sums[2],
    )


def solution(mesh):
    return jax.shard_map(
        body,
        mesh=mesh,
        in_specs=(
            P(("dp", "fsdp"), None),
            P(("dp", "fsdp"), None),
            P(("dp", "fsdp"), None),
            P(("dp", "fsdp"), None),
            P(("dp", "fsdp"), None),
            P(("dp", "fsdp")),
            P(("dp", "fsdp")),
            P(("dp", "fsdp"), None),
            P("dp", None),
            P("dp", None, None),
            P("dp", None, None),
        ),
        out_specs=(
            P(("dp", "fsdp"), None),
            P(("dp", "fsdp"), None),
            P(("dp", "fsdp"), None),
            P(("dp", "fsdp"), None),
            P(("dp", "fsdp"), None),
            P(("dp", "fsdp"), None),
            P(("dp", "fsdp")),
            P(("dp", "fsdp")),
        ),
        check_vma=False,
    )
```

profile of v0, /device:TPU:1, one launch (start us, length us, event | category | flops | bytes accessed | tf_op | source)
XLA Modules:
  0.0 4571.2 jit_solution(8496526743868702310)
XLA Ops:
  9.7 42.3 all-reduce.5
  55.0 114.3 %all-gather.9.cloned.1.call-done = bf16[2048,6144]{1,0:T(8,128)(2,1)} async-done(((bf16[64,6144]{1,0:T(8,128)(2,1)}), bf16[2048,6144]{1,0:T(8,128)(2,1)}) %all-gather.9.cloned.1.call-update) | async-done | bytes 25165840 | tf_op jit(solution)/shard_map/all_gather | solution.py:235
  169.3 10.3 fusion.75
  185.1 1.7 copy.96
  192.7 58.0 %all-gather.13.cloned.1.call-done = bf16[1024,2048]{1,0:T(8,128)(2,1)} async-done(((bf16[128,2048]{1,0:T(8,128)(2,1)}), bf16[1024,2048]{1,0:T(8,128)(2,1)}) %all-gather.13.cloned.1.call-update) | async-done | bytes 4194320 | tf_op jit(solution)/shard_map/all_gather | solution.py:244
  250.7 5.7 copy.109
  256.4 71.0 %all-gather.11.cloned.1.call-done = bf16[1024,2048]{0,1:T(8,128)(2,1)} async-done(((bf16[128,2048]{0,1:T(8,128)(2,1)}), bf16[1024,2048]{0,1:T(8,128)(2,1)}) %all-gather.11.cloned.1.call-update) | async-done | bytes 4194320 | tf_op jit(solution)/shard_map/all_gather | solution.py:243
  327.4 6.8 conditional.4
  327.4 4.2 fusion
  331.5 2.6 select_reduce_fusion
  334.3 7.4 conditional.5
  334.5 7.2 fusion.9
  342.8 64.1 %all-gather.15.cloned.1.call-done = bf16[2048,2048]{1,0:T(8,128)(2,1)} async-done(((bf16[64,2048]{1,0:T(8,128)(2,1)}), bf16[2048,2048]{1,0:T(8,128)(2,1)}) %all-gather.15.cloned.1.call-update) | async-done | bytes 8388624 | tf_op jit(solution)/shard_map/all_gather | solution.py:236
  406.9 5.0 fusion.88
  412.2 191.0 %all-gather.19.cloned.1.call-done = bf16[8192,2048]{1,0:T(8,128)(2,1)} async-done(((bf16[256,2048]{1,0:T(8,128)(2,1)}), bf16[8192,2048]{1,0:T(8,128)(2,1)}) %all-gather.19.cloned.1.call-update) | async-done | bytes 33554448 | tf_op jit(solution)/shard_map/all_gather | solution.py:251
  603.1 18.1 fusion.89
  621.3 177.7 %all-gather.17.cloned.1.call-done = bf16[2048,8192]{1,0:T(8,128)(2,1)} async-done(((bf16[64,8192]{1,0:T(8,128)(2,1)}), bf16[2048,8192]{1,0:T(8,128)(2,1)}) %all-gather.17.cloned.1.call-update) | async-done | bytes 33554448 | tf_op jit(solution)/shard_map/all_gather | solution.py:250
  799.0 18.2 fusion.52
  817.2 17.3 multiply_reduce_fusion
  836.1 6.7 convolution_convert_fusion
  845.1 9.3 fusion.90
  856.0 26.0 all_gather.56
  882.0 26.7 all_gather.57
  908.7 2.6 multiply_reduce_fusion.1
  912.1 1.9 copy.110
  914.0 28.9 conditional.6
  914.0 8.4 fusion.34
  923.1 11.9 fusion.41
  934.9 3.3 fusion.85
  938.2 2.3 copy.104
  940.6 2.4 copy.105
  942.9 32.0 all_gather.59
  974.9 25.5 conditional.7
  975.1 9.2 divide_select_fusion
  985.5 8.8 fusion.29
  994.3 6.2 fusion.24
  1001.5 1.6 copy.80
  1003.1 1.5 add_convert_fusion.2
  1004.7 21.1 fusion.65
  1026.5 25.1 fusion.80
  1051.9 25.8 fusion.82
  1077.7 17.9 fusion.53
  1095.6 13.8 fusion.63
  1110.0 66.3 %all-reduce.4 = (f32[2048]{0:T(1024)S(1)}, f32[2048]{0:T(1024)S(1)}) all-reduce(f32[2048]{0:T(1024)S(1)} %get-tuple-element.504, f32[2048]{0:T(1024)S(1)} %copy-done.19), channel_id=6, replica_groups=mesh['dp'=4,'fsdp'=8] {'dp','fsdp'}, use_global_device_ids=true, to_apply=%region_27.28.clone | all-reduce | flops 4096 | bytes 32768
  1178.8 137.8 %reduce-scatter.7.cloned.1.call-done = f32[64,2048]{1,0:T(8,128)} async-done(((f32[2048,2048]{1,0:T(8,128)}), f32[64,2048]{1,0:T(8,128)}) %reduce-scatter.7.cloned.1.call-update) | async-done | bytes 524304 | tf_op jit(solution)/shard_map/reduce_scatter | solution.py:396
  1316.6 437.8 %reduce-scatter.5.cloned.1.call-done = f32[64,6144]{1,0:T(8,128)} async-done(((f32[2048,6144]{1,0:T(8,128)}), f32[64,6144]{1,0:T(8,128)}) %reduce-scatter.5.cloned.1.call-update) | async-done | bytes 1572880 | tf_op jit(solution)/shard_map/reduce_scatter | solution.py:395
  1754.4 1404.5 %reduce-scatter.9.cloned.1.call-done = f32[64,8192]{1,0:T(8,128)} async-done(((f32[2048,8192]{1,0:T(8,128)}), f32[64,8192]{1,0:T(8,128)}) %reduce-scatter.9.cloned.1.call-update) | async-done | bytes 2097168 | tf_op jit(solution)/shard_map/reduce_scatter | solution.py:306
  3158.9 1405.3 %reduce-scatter.11.cloned.1.call-done = f32[256,2048]{1,0:T(8,128)} async-done(((f32[8192,2048]{1,0:T(8,128)}), f32[256,2048]{1,0:T(8,128)}) %reduce-scatter.11.cloned.1.call-update) | async-done | bytes 2097168 | tf_op jit(solution)/shard_map/reduce_scatter | solution.py:307
  (142 shorter events, 28.6 us)
Async XLA Ops:
  7.2 162.2 %all-gather.9.cloned.1.call-start = ((), (), s32[]{:S(2)}) async-start(), calls=%async_computation.4 | async-start | bytes 25952256 | tf_op jit(solution)/shard_map/all_gather | solution.py:235
  7.9 242.8 %all-gather.13.cloned.1.call-start = ((), (), s32[]{:S(2)}) async-start(), calls=%async_computation.6 | async-start | bytes 4718592 | tf_op jit(solution)/shard_map/all_gather | solution.py:244
  51.9 127.7 %copy-start.12 = (f32[2048]{0:T(1024)}, f32[2048]{0:T(1024)S(1)}, u32[]{:S(2)}) copy-start(f32[2048]{0:T(1024)S(1)} %convert_element_type.149) | copy-start | bytes 24580
  53.1 126.5 %copy-start.15 = (f32[128]{0:T(128)}, f32[128]{0:T(128)S(1)}, u32[]{:S(2)}) copy-start(f32[128]{0:T(128)S(1)} %broadcast_multiply_fusion.1) | copy-start | bytes 1540
  54.5 0.5 copy-start.29
  55.0 124.7 %copy-start.17 = (f32[128]{0:T(128)}, f32[128]{0:T(128)S(1)}, u32[]{:S(2)}) copy-start(f32[128]{0:T(128)S(1)} %fusion.70) | copy-start | bytes 1540
  55.0 125.6 %copy-start.26 = (s32[1,2,4]{2,1,0:T(2,128)S(1)}, s32[1,2,4]{2,1,0:T(2,128)}, u32[]{:S(2)}) copy-start(s32[1,2,4]{2,1,0:T(2,128)} %param.29) | copy-start | bytes 100
  55.0 125.6 %copy-start.27 = (s32[1,2,4]{2,1,0:T(2,128)S(1)}, s32[1,2,4]{2,1,0:T(2,128)}, u32[]{:S(2)}) copy-start(s32[1,2,4]{2,1,0:T(2,128)} %param.28) | copy-start | bytes 100
  55.0 125.6 %copy-start.28 = (s32[1,2]{1,0:T(1,128)S(1)}, s32[1,2]{1,0:T(1,128)}, u32[]{:S(2)}) copy-start(s32[1,2]{1,0:T(1,128)} %param.27) | copy-start | bytes 28
  180.5 146.8 %all-gather.11.cloned.1.call-start = ((), (), s32[]{:S(2)}) async-start(), calls=%async_computation.5 | async-start | bytes 4718592 | tf_op jit(solution)/shard_map/all_gather | solution.py:243
  185.1 6.1 copy-start.9
  187.9 219.0 %all-gather.15.cloned.1.call-start = ((), (), s32[]{:S(2)}) async-start(), calls=%async_computation.7 | async-start | bytes 8650752 | tf_op jit(solution)/shard_map/all_gather | solution.py:236
  188.4 414.7 %all-gather.19.cloned.1.call-start = ((), (), s32[]{:S(2)}) async-start(), calls=%async_computation.9 | async-start | bytes 34603008 | tf_op jit(solution)/shard_map/all_gather | solution.py:251
  189.0 610.0 %all-gather.17.cloned.1.call-start = ((), (), s32[]{:S(2)}) async-start(), calls=%async_computation.8 | async-start | bytes 34603008 | tf_op jit(solution)/shard_map/all_gather | solution.py:250
  189.6 785.3 %all-gather.21.cloned.1.call-start = ((), (), s32[]{:S(2)}) async-start(), calls=%async_computation.10 | async-start | bytes 4718592 | tf_op jit(solution)/shard_map/all_gather | solution.py:332
  192.6 782.3 %all-gather.23.cloned.1.call-start = ((), (), s32[]{:S(2)}) async-start(), calls=%async_computation.11 | async-start | bytes 4718592 | tf_op jit(solution)/shard_map/all_gather | solution.py:333
  250.7 76.7 %copy-start.8 = (bf16[128,16,128]{0,2,1:T(8,128)(2,1)S(1)}, bf16[128,16,128]{0,2,1:T(8,128)(2,1)}, u32[]{:S(2)}) copy-start(bf16[128,16,128]{0,2,1:T(8,128)(2,1)} %pad_maximum_fusion.3) | copy-start | bytes 1572868
  334.1 547.9 %copy-start.14 = (f32[16,128]{1,0:T(8,128)}, f32[16,128]{1,0:T(8,128)S(1)}, u32[]{:S(2)}) copy-start(f32[16,128]{1,0:T(8,128)S(1)} %get-tuple-element.407) | copy-start | bytes 24580
  334.2 72.6 %copy-start = (bf16[128,2048]{1,0:T(8,128)(2,1)S(1)}, bf16[128,2048]{1,0:T(8,128)(2,1)}, u32[]{:S(2)}) copy-start(bf16[128,2048]{1,0:T(8,128)(2,1)} %param.19) | copy-start | bytes 1572868
  341.7 65.2 %copy-start.4 = (f32[128,16,128]{2,0,1:T(8,128)}, f32[128,16,128]{2,0,1:T(8,128)S(1)}, u32[]{:S(2)}) copy-start(f32[128,16,128]{2,0,1:T(8,128)S(1)} %get-tuple-element.560) | copy-start | bytes 3145732
  406.9 196.3 %copy-start.5 = (bf16[128,2048]{1,0:T(8,128)(2,1)S(1)}, bf16[128,2048]{1,0:T(8,128)(2,1)}, u32[]{:S(2)}) copy-start(bf16[128,2048]{1,0:T(8,128)(2,1)} %param.26) | copy-start | bytes 1572868
  411.9 422.7 %copy-start.20 = (f32[128]{0:T(128)}, f32[128]{0:T(128)S(1)}, u32[]{:S(2)}) copy-start(f32[128]{0:T(128)S(1)} %broadcast_multiply_fusion) | copy-start | bytes 1540
  412.1 422.4 %copy-start.22 = (f32[128]{0:T(128)}, f32[128]{0:T(128)S(1)}, u32[]{:S(2)}) copy-start(f32[128]{0:T(128)S(1)} %fusion.71) | copy-start | bytes 1540
  817.2 17.3 copy-start.1
  835.0 1.0 copy-start.2
  835.0 7.9 copy-start.24
  836.1 6.7 copy-start.7
  842.9 0.8 copy-start.6
  844.6 471.9 %reduce-scatter.7.cloned.1.call-start = ((), (), s32[]{:S(2)}) async-start(), calls=%async_computation.13 | async-start | bytes 17301504 | tf_op jit(solution)/shard_map/reduce_scatter | solution.py:396
  854.4 900.0 %reduce-scatter.5.cloned.1.call-start = ((), (), s32[]{:S(2)}) async-start(), calls=%async_computation.12 | async-start | bytes 51904512 | tf_op jit(solution)/shard_map/reduce_scatter | solution.py:395
  1000.5 4.2 copy-start.13
  1000.5 4.2 copy-start.16
  1000.5 4.2 copy-start.18
  1004.6 21.2 copy-start.10
  1004.7 21.2 copy-start.11
  1025.8 0.6 copy-start.21
  1025.8 0.7 copy-start.23
  1025.9 2133.0 %reduce-scatter.9.cloned.1.call-start = ((), (), s32[]{:S(2)}) async-start(), calls=%async_computation.14 | async-start | bytes 69206016 | tf_op jit(solution)/shard_map/reduce_scatter | solution.py:306
  1051.6 3512.5 %reduce-scatter.11.cloned.1.call-start = ((), (), s32[]{:S(2)}) async-start(), calls=%async_computation.15 | async-start | bytes 69206016 | tf_op jit(solution)/shard_map/reduce_scatter | solution.py:307
  1095.6 13.8 copy-start.30
  1095.6 14.4 copy-start.19
  1095.6 81.8 %copy-start.3 = (f32[128,2048]{1,0:T(8,128)S(1)}, f32[128,2048]{1,0:T(8,128)}, u32[]{:S(2)}) copy-start(f32[128,2048]{1,0:T(8,128)} %copy-done.2) | copy-start | bytes 3145732
  1095.6 81.8 %copy-start.25 = (f32[128]{0:T(128)S(1)}, f32[128]{0:T(128)}, u32[]{:S(2)}) copy-start(f32[128]{0:T(128)} %copy-done.24) | copy-start | bytes 1540
Sparse Core Ops, SparseCore 0:
  10.9 158.3 all-gather.8
  180.7 69.9 all-gather.12
  253.3 74.0 all-gather.10
  330.2 76.6 all-gather.14
  409.7 193.3 all-gather.18
  606.0 192.9 all-gather.16
  801.6 72.7 all-gather.20
  876.5 72.2 all-gather.22
  951.7 364.8 reduce-scatter.6
  1323.4 430.9 reduce-scatter.4
  1757.3 1401.4 reduce-scatter.8
  3161.6 1402.4 reduce-scatter.10
where the time goes:
time: 4580 us; the launch traced here: 4570 us
  waiting for transfers between devices  4060 us (89%)
  matrix products  244 us (5%)
  blocking collectives  193 us (4%)
    reduce_scatter x1, waiting for transfers between devices, body(): lax.psum_scatter(down_term, ('dp', 'fsdp'), scatter_dimension=0, tiled=True)  1410 us
    reduce_scatter x1, waiting for transfers between devices, body(): lax.psum_scatter(up_term, ('dp', 'fsdp'), scatter_dimension=0, tiled=True)  1400 us
    reduce_scatter x1, waiting for transfers between devices, body(): lax.psum_scatter(triple_term, ('dp', 'fsdp'), scatter_dimension=0, tiled=...  438 us
    all_gather x1, waiting for transfers between devices, body(): lax.all_gather(down_weight, ('dp', 'fsdp'), axis=0, tiled=True)  191 us
    all_gather x1, waiting for transfers between devices, body(): lax.all_gather(up_weight, ('dp', 'fsdp'), axis=0, tiled=True)  178 us
    reduce_scatter x1, waiting for transfers between devices, body(): lax.psum_scatter(output_term, ('dp', 'fsdp'), scatter_dimension=0, tiled=...  138 us
    all_gather x1, waiting for transfers between devices, body(): lax.all_gather(triple_weight, ('dp', 'fsdp'), axis=0, tiled=True)  114 us
    unnamed x2, blocking collectives  109 us
  transfers between devices with their start and end apart: 12, of which 10 were waited for; matrix products, arithmetic and copies ran while one was open for 6% of the time, Pallas kernels for 0%

commit v1 on v0

--- a/solution.py
+++ b/solution.py
@@ -3,6 +3,8 @@
 import jax
 import jax.numpy as jnp
 from jax import lax
+from jax.experimental import pallas as pl
+from jax.experimental.pallas import tpu as pltpu
 from jax.sharding import PartitionSpec as P
 
 HEADS = 16
@@ -200,7 +202,7 @@
     return (result, attended_low, middle, normed_two, hidden, activation)
 
 
-def body(
+def whole_rows_body(
     tokens,
     triple_weight,
     output_weight,
@@ -408,32 +410,486 @@
     )
 
 
+AXES = ("dp", "fsdp")
+DEVICES = 32
+GROUPS = 4
+MEMBERS = 8
+CORE, ZL, Y = 8, 2, 1
+X, ZH = 16, 4
+BF16 = jnp.bfloat16
+F32 = jnp.float32
+SMEM = pl.BlockSpec(memory_space=pltpu.SMEM)
+VMEM = pl.BlockSpec(memory_space=pltpu.VMEM)
+HBM = pl.BlockSpec(memory_space=pltpu.HBM)
+
+
+def swap(array, bits):
+    return lax.ppermute(array, AXES, [(i, i ^ bits) for i in range(DEVICES)])
+
+
+def member_bits(k):
+    return (k >> 2) * CORE + ((k >> 1) & 1) * ZL + (k & 1) * Y
+
+
+def regroup_pairs():
+    def target(i):
+        x, core, zh, low = i >> 4, (i >> 3) & 1, (i >> 2) & 1, i & 3
+        return (x << 4) | (zh << 3) | (core << 2) | low
+
+    return [(i, target(i)) for i in range(DEVICES)]
+
+
+def regroup(array):
+    return lax.ppermute(array, AXES, regroup_pairs())
+
+
+def output_pairs(a, b):
+    def target(i):
+        x, core, zh, zl, y = i >> 4, (i >> 3) & 1, (i >> 2) & 1, (i >> 1) & 1, i & 1
+        return ((y ^ a) << 4) | (core << 3) | ((zh ^ b) << 2) | (zl << 1) | x
+
+    return [(i, target(i)) for i in range(DEVICES)]
+
+
+def gather_members(own):
+    near = [own, swap(own, Y), swap(own, ZL), swap(own, ZL | Y)]
+    far = [swap(part, CORE) for part in near]
+    return jnp.concatenate(near + far, axis=0)
+
+
+def scatter_members(left, right):
+    half = left.shape[0] // 2
+    rows = half // 4
+    far = jnp.dot(left[half:], right, preferred_element_type=F32).astype(BF16)
+    far = swap(far, CORE)
+    near = jnp.dot(left[:half], right, preferred_element_type=F32).astype(BF16)
+    total = [
+        near[i * rows : (i + 1) * rows].astype(F32) + far[i * rows : (i + 1) * rows].astype(F32)
+        for i in range(4)
+    ]
+    sent = [swap(total[i].astype(BF16), member_bits(i)) for i in (3, 1, 2)]
+    return total[0] + sent[0].astype(F32) + sent[1].astype(F32) + sent[2].astype(F32)
+
+
+def hidden_columns(member, width):
+    core, zl, y = (member >> 2) & 1, (member >> 1) & 1, member & 1
+    return [
+        ((gx * X + core * CORE + gz * ZH + zl * ZL + y) * width, width)
+        for gx in range(2)
+        for gz in range(2)
+    ]
+
+
+def head_columns(member, width):
+    core, zl, y = (member >> 2) & 1, (member >> 1) & 1, member & 1
+    return [
+        (part * width + ((y * 2 + core) * 4 + half * 2 + zl) * HEAD, HEAD)
+        for part in range(3)
+        for half in range(2)
+    ]
+
+
+def deal_columns(member, own, columns):
+    rows = own.shape[0]
+    width = own.shape[1] // MEMBERS
+
+    def kernel(member_ref, own_ref, *slabs):
+        for k in range(MEMBERS):
+            start = 0
+            for place, size in columns(member_ref[0] ^ k):
+                slabs[k][:, start : start + size] = own_ref[:, pl.ds(pl.multiple_of(place, 128), size)]
+                start += size
+
+    return pl.pallas_call(
+        kernel,
+        out_shape=[jax.ShapeDtypeStruct((rows, width), own.dtype)] * MEMBERS,
+        in_specs=[SMEM, VMEM],
+        out_specs=[VMEM] * MEMBERS,
+    )(member, own)
+
+
+def place_rows(places, pieces, blocks):
+    rows = pieces[0].shape[0] // blocks
+    width = pieces[0].shape[1]
+    total = len(pieces) * blocks
+
+    def kernel(places_ref, *rest):
+        piece_refs, whole_ref, sems = rest[: len(pieces)], rest[len(pieces)], rest[len(pieces) + 1]
+        copies = [
+            pltpu.make_async_copy(
+                piece_refs[i // blocks].at[pl.ds(i % blocks * rows, rows)],
+                whole_ref.at[pl.ds(pl.multiple_of(places_ref[i] * rows, rows), rows)],
+                sems.at[i],
+            )
+            for i in range(total)
+        ]
+        for copy in copies:
+            copy.start()
+        for copy in copies:
+            copy.wait()
+
+    return pl.pallas_call(
+        kernel,
+        out_shape=jax.ShapeDtypeStruct((total * rows, width), pieces[0].dtype),
+        in_specs=[SMEM] + [HBM] * len(pieces),
+        out_specs=VMEM,
+        scratch_shapes=[pltpu.SemaphoreType.DMA((total,))],
+        compiler_params=pltpu.CompilerParams(vmem_limit_bytes=16 << 20),
+    )(places, *pieces)
+
+
+def gather_columns(member, own, columns, places):
+    slabs = deal_columns(member, own, columns)
+    parts = [slabs[0]] + [swap(slabs[k], member_bits(k)) for k in range(1, MEMBERS)]
+    group = jnp.concatenate(parts, axis=0)
+    other = swap(group, ZH)
+    return place_rows(places, [group, other, swap(group, X), swap(other, X)], MEMBERS)
+
+
+def gather_gains(device, own):
+    whole = own[None]
+    for bits in (Y, ZL, CORE, ZH, X):
+        other = swap(whole, bits)
+        whole = jnp.where((device & bits) == 0, jnp.concatenate([whole, other]), jnp.concatenate([other, whole]))
+    order = whole.reshape(2, 2, 2, 2, 2, 2, -1)
+    return order.transpose(5, 0, 2, 1, 3, 4, 6).reshape(2, -1).astype(F32)
+
+
+def deal_sums(member, kept, came):
+    rows = kept.shape[0] // MEMBERS
+    width = kept.shape[1]
+
+    def kernel(member_ref, kept_ref, came_ref, *slabs):
+        for k in range(MEMBERS):
+            block = pl.ds(pl.multiple_of((member_ref[0] ^ k) * rows, rows), rows)
+            slabs[k][...] = (kept_ref[block, :].astype(F32) + came_ref[block, :].astype(F32)).astype(BF16)
+
+    return pl.pallas_call(
+        kernel,
+        out_shape=[jax.ShapeDtypeStruct((rows, width), BF16)] * MEMBERS,
+        in_specs=[SMEM, VMEM, VMEM],
+        out_specs=[VMEM] * MEMBERS,
+        compiler_params=pltpu.CompilerParams(vmem_limit_bytes=32 << 20),
+    )(member, kept, came)
+
+
+def place_columns(member, parts, columns):
+    rows, width = parts[0].shape
+
+    def kernel(member_ref, *rest):
+        part_refs, whole_ref = rest[:MEMBERS], rest[MEMBERS]
+        for k in range(MEMBERS):
+            start = 0
+            for place, size in columns(member_ref[0] ^ k):
+                whole_ref[:, pl.ds(pl.multiple_of(place, 128), size)] = part_refs[k][
+                    :, start : start + size
+                ].astype(F32)
+                start += size
+
+    return pl.pallas_call(
+        kernel,
+        out_shape=jax.ShapeDtypeStruct((rows, width * MEMBERS), F32),
+        in_specs=[SMEM] + [VMEM] * MEMBERS,
+        out_specs=VMEM,
+        compiler_params=pltpu.CompilerParams(vmem_limit_bytes=32 << 20),
+    )(member, *parts)
+
+
+def scatter_columns(member, x, zh, grad, columns):
+    width = grad.shape[1]
+    quarter = grad.shape[0] // 8
+    blocks = grad.reshape(2, 2, 2, quarter, width)
+    came = swap(lax.dynamic_index_in_dim(blocks, 1 - x, 0, False), X)
+
+    def half_sum(which):
+        mine = lax.dynamic_slice(blocks, (x, 0, which, 0, 0), (1, 2, 1, quarter, width))
+        theirs = lax.dynamic_slice(came, (0, which, 0, 0), (2, 1, quarter, width))
+        total = mine.reshape(2 * quarter, width).astype(F32) + theirs.reshape(2 * quarter, width).astype(F32)
+        return total.astype(BF16)
+
+    far = swap(half_sum(1 - zh), ZH)
+    slabs = deal_sums(member, half_sum(zh), far)
+    parts = [slabs[0]] + [swap(slabs[k], member_bits(k)) for k in range(1, MEMBERS)]
+    return place_columns(member, parts, columns)
+
+
+def scatter_rows(x, zh, grad):
+    rows, width = grad.shape[0] // 4, grad.shape[1]
+    blocks = grad.reshape(2, 2, rows, width)
+    came = swap(lax.dynamic_index_in_dim(blocks, 1 - x, 0, False), X)
+
+    def half_sum(which):
+        mine = lax.dynamic_slice(blocks, (x, which, 0, 0), (1, 1, rows, width)).reshape(rows, width)
+        theirs = lax.dynamic_index_in_dim(came, which, 0, False)
+        return mine.astype(F32) + theirs.astype(F32)
+
+    return half_sum(zh) + swap(half_sum(1 - zh).astype(BF16), ZH).astype(F32)
+
+
+def turn(vectors, cosine, sine):
+    return vectors * cosine + pltpu.roll(vectors, HEAD // 2, 1) * sine
+
+
+def key_place_row(member, rows):
+    lane = lax.broadcasted_iota(jnp.int32, (1, rows), 1)
+    return jnp.concatenate([lane + (member ^ k) * rows for k in range(MEMBERS)], axis=1)
+
+
+def block_mask(layout_ref, block, block_rows, rows, key_place):
+    member, first_end, second_end = layout_ref[0], layout_ref[1], layout_ref[2]
+    per_block = block_rows // rows
+    row = lax.broadcasted_iota(jnp.int32, (rows, 1), 0)
+    place = jnp.concatenate(
+        [row + (member ^ (block * per_block + i)) * rows for i in range(per_block)], axis=0
+    )
+    start = jnp.where(place < first_end, 0, jnp.where(place < second_end, first_end, second_end))
+    return (key_place <= place) & (key_place >= start)
+
+
+def masked_probs(queries, keys, allowed):
+    scores = lax.dot_general(queries, keys, (((1,), (1,)), ((), ())), preferred_element_type=F32)
+    scores = jnp.where(allowed, scores * HEAD ** (-0.5), MASKED)
+    weights = jnp.exp(scores - jnp.max(scores, axis=-1, keepdims=True))
+    return weights * (1.0 / jnp.sum(weights, axis=-1, keepdims=True))
+
+
+BLOCK = 256
+
+
+def attention_forward(layout, mixed, cosine, sine):
+    count = mixed.shape[0]
+    width = mixed.shape[1] // 3
+    rows = count // MEMBERS
+
+    def kernel(layout_ref, mixed_ref, cos_ref, sin_ref, q_ref, k_ref, v_ref, out_ref):
+        key_place = key_place_row(layout_ref[0], rows)
+        v_ref[...] = mixed_ref[:, 2 * width :].astype(BF16)
+        for head in range(width // HEAD):
+            span = slice(head * HEAD, (head + 1) * HEAD)
+            key_span = slice(width + head * HEAD, width + (head + 1) * HEAD)
+            q_ref[:, span] = turn(mixed_ref[:, span], cos_ref[...], sin_ref[...]).astype(BF16)
+            k_ref[:, span] = turn(mixed_ref[:, key_span], cos_ref[...], sin_ref[...]).astype(BF16)
+
+        @pl.loop(0, count // BLOCK)
+        def _(block):
+            here = pl.ds(pl.multiple_of(block * BLOCK, BLOCK), BLOCK)
+            allowed = block_mask(layout_ref, block, BLOCK, rows, key_place)
+            for head in range(width // HEAD):
+                span = slice(head * HEAD, (head + 1) * HEAD)
+                probs = masked_probs(q_ref[here, span], k_ref[:, span], allowed)
+                out_ref[here, span] = jnp.dot(
+                    probs.astype(BF16), v_ref[:, span], preferred_element_type=F32
+                ).astype(BF16)
+
+    return pl.pallas_call(
+        kernel,
+        out_shape=[jax.ShapeDtypeStruct((count, width), BF16)] * 4,
+        in_specs=[SMEM, VMEM, VMEM, VMEM],
+        out_specs=[VMEM] * 4,
+        compiler_params=pltpu.CompilerParams(vmem_limit_bytes=48 << 20),
+    )(layout, mixed, cosine, sine)
+
+
+def attention_backward_heads(layout, queries, keys, values, grad_out, cosine, sine):
+    count, width = queries.shape
+    rows = count // MEMBERS
+
+    def kernel(layout_ref, q_ref, k_ref, v_ref, g_ref, cos_ref, sin_ref, out_ref, gk_ref, gv_ref):
+        key_place = key_place_row(layout_ref[0], rows)
+        gk_ref[...] = jnp.zeros_like(gk_ref)
+        gv_ref[...] = jnp.zeros_like(gv_ref)
+
+        @pl.loop(0, count // BLOCK)
+        def _(block):
+            here = pl.ds(pl.multiple_of(block * BLOCK, BLOCK), BLOCK)
+            allowed = block_mask(layout_ref, block, BLOCK, rows, key_place)
+            for head in range(width // HEAD):
+                span = slice(head * HEAD, (head + 1) * HEAD)
+                q, g = q_ref[here, span], g_ref[here, span]
+                probs = masked_probs(q, k_ref[:, span], allowed)
+                grad_probs = lax.dot_general(
+                    g, v_ref[:, span], (((1,), (1,)), ((), ())), preferred_element_type=F32
+                )
+                delta = jnp.sum(probs * grad_probs, axis=-1, keepdims=True)
+                grad_scores = (probs * (grad_probs - delta)).astype(BF16)
+                grad_query = jnp.dot(grad_scores, k_ref[:, span], preferred_element_type=F32)
+                out_ref[here, span] = turn(
+                    grad_query * HEAD ** (-0.5), cos_ref[here, :], -sin_ref[here, :]
+                ).astype(BF16)
+                over_rows = (((0,), (0,)), ((), ()))
+                gk_ref[:, span] += lax.dot_general(grad_scores, q, over_rows, preferred_element_type=F32)
+                gv_ref[:, span] += lax.dot_general(
+                    probs.astype(BF16), g, over_rows, preferred_element_type=F32
+                )
+
+        out_ref[:, 2 * width :] = gv_ref[...].astype(BF16)
+        for head in range(width // HEAD):
+            span = slice(head * HEAD, (head + 1) * HEAD)
+            out_ref[:, width + head * HEAD : width + (head + 1) * HEAD] = turn(
+                gk_ref[:, span] * HEAD ** (-0.5), cos_ref[...], -sin_ref[...]
+            ).astype(BF16)
+
+    return pl.pallas_call(
+        kernel,
+        out_shape=jax.ShapeDtypeStruct((count, 3 * width), BF16),
+        in_specs=[SMEM] + [VMEM] * 6,
+        out_specs=VMEM,
+        scratch_shapes=[pltpu.VMEM((count, width), F32), pltpu.VMEM((count, width), F32)],
+        compiler_params=pltpu.CompilerParams(vmem_limit_bytes=48 << 20),
+    )(layout, queries, keys, values, grad_out, cosine, sine)
+
+
+def norm_parts(values):
+    centred = values - jnp.mean(values, axis=-1, keepdims=True)
+    inverse = lax.rsqrt(jnp.mean(centred * centred, axis=-1, keepdims=True) + EPSILON)
+    return centred * inverse, inverse
+
+
+def norm_backward(values, gain, grad):
+    normal, inverse = norm_parts(values)
+    scaled = grad * gain
+    return inverse * (
+        scaled
+        - jnp.mean(scaled, axis=-1, keepdims=True)
+        - normal * jnp.mean(scaled * normal, axis=-1, keepdims=True)
+    )
+
+
+def contract_rows(left, right):
+    return lax.dot_general(left, right, (((0,), (0,)), ((), ())), preferred_element_type=F32)
+
+
+def dot_transposed(left, right):
+    return lax.dot_general(left, right, (((1,), (1,)), ((), ())), preferred_element_type=F32)
+
+
+def grouped_body(
+    tokens,
+    triple_weight,
+    output_weight,
+    up_weight,
+    down_weight,
+    first_gain,
+    second_gain,
+    cotangent,
+    frame_counts,
+    text_counts,
+    action_counts,
+):
+    rows, width = tokens.shape
+    count = rows * MEMBERS
+    dp, fsdp = lax.axis_index("dp"), lax.axis_index("fsdp")
+    x, core = dp >> 1, dp & 1
+    zh, low = fsdp >> 2, fsdp & 3
+    device = dp * 8 + fsdp
+    member = core * 4 + low
+    member_array = member.reshape(1)
+
+    hidden_width = up_weight.shape[1] // DEVICES
+    source_bits = jnp.array(
+        [group ^ member_bits(k) for group in (0, ZH, X, X | ZH) for k in range(MEMBERS)], jnp.int32
+    )
+    row_places = device ^ source_bits
+    group_index = x * 2 + zh
+    group_places = group_index ^ jnp.arange(GROUPS, dtype=jnp.int32)
+    triple_columns = lambda m: head_columns(m, width)
+    up_columns = lambda m: hidden_columns(m, hidden_width)
+
+    tokens = regroup(tokens)
+    triple = gather_columns(member_array, triple_weight, triple_columns, row_places)
+    all_tokens = gather_members(tokens)
+    gains = gather_gains(device, jnp.stack([first_gain, second_gain]))
+
+    output_parts = [lax.ppermute(output_weight, AXES, output_pairs(a, b)) for a in (0, 1) for b in (0, 1)]
+    output_places = jnp.stack([(zh ^ b) * 2 + (x ^ a) for a in (0, 1) for b in (0, 1)])
+    output = place_rows(output_places, output_parts, 1)
+
+    up = gather_columns(member_array, up_weight, up_columns, row_places)
+    down_other = swap(down_weight, ZH)
+    down = place_rows(
+        group_places, [down_weight, down_other, swap(down_weight, X), swap(down_other, X)], 1
+    )
+    cotangent = regroup(cotangent)
+    all_cotangent = gather_members(cotangent)
+
+    counts = jnp.concatenate(
+        [frame_counts.reshape(-1), text_counts.reshape(-1), action_counts.reshape(-1)]
+    )
+    counts = jnp.where(core == zh, counts, swap(counts, CORE))
+    frames = counts[:2]
+    slots = text_counts.shape[-1]
+    texts = counts[2 : 2 + 2 * slots].reshape(2, slots)
+    actions = counts[2 + 2 * slots :].reshape(2, slots)
+    live = jnp.arange(slots, dtype=jnp.int32) < frames[:, None]
+    lengths = jnp.sum(jnp.where(live, IMG + texts + actions, 0), axis=-1)
+    first_end = lengths[0]
+    second_end = lengths[0] + lengths[1]
+    layout = jnp.stack([member, first_end, second_end]).astype(jnp.int32)
+    block_order = member ^ jnp.arange(MEMBERS, dtype=jnp.int32)
+    places = (block_order[:, None] * rows + jnp.arange(rows, dtype=jnp.int32)[None, :]).reshape(-1)
+    starts = jnp.where(places < first_end, 0, jnp.where(places < second_end, first_end, second_end))
+    cosine, sine = rotary_tables(places - starts)
+    cosine = jnp.concatenate([cosine[:, 0], cosine[:, 0]], axis=1)
+    sine = jnp.concatenate([-sine[:, 0], sine[:, 0]], axis=1)
+
+    normed = norm_rows(all_tokens.astype(F32), gains[0]).astype(BF16)
+    mixed = jnp.dot(normed, triple, preferred_element_type=F32)
+    queries, keys, values, attended = attention_forward(layout, mixed, cosine, sine)
+    inputs = tokens.astype(F32)
+    middle = inputs + scatter_members(attended, output)
+    normed_two = gather_members(norm_rows(middle, gains[1]).astype(BF16))
+    hidden = jnp.dot(normed_two, up, preferred_element_type=F32)
+    activation, gelu_pull = jax.vjp(jax.nn.gelu, hidden)
+    activation = activation.astype(BF16)
+    grad_hidden = gelu_pull(dot_transposed(all_cotangent, down))[0].astype(BF16)
+
+    grad_normed_two = scatter_members(grad_hidden, up.T)
+    grad_middle = cotangent.astype(F32) + norm_backward(middle, gains[1], grad_normed_two)
+    grad_branch = gather_members(grad_middle.astype(BF16))
+    grad_attended = dot_transposed(grad_branch, output).astype(BF16)
+    grad_mixed = attention_backward_heads(layout, queries, keys, values, grad_attended, cosine, sine)
+    grad_normed = scatter_members(grad_mixed, triple.T)
+    token_grad = grad_middle + norm_backward(inputs, gains[0], grad_normed)
+    token_grad = regroup(token_grad.astype(BF16))
+
+    layer_output = middle + scatter_members(activation, down)
+    layer_output = regroup(layer_output.astype(BF16))
+
+    down_grad = scatter_rows(x, zh, contract_rows(activation, all_cotangent).astype(BF16))
+    up_grad = scatter_columns(
+        member_array, x, zh, contract_rows(normed_two, grad_hidden).astype(BF16), up_columns
+    )
+    output_term = contract_rows(attended, grad_branch).astype(BF16).reshape(GROUPS, -1, width)
+    output_grad = 0.0
+    for a in (0, 1):
+        for b in (0, 1):
+            piece = lax.dynamic_index_in_dim(output_term, (zh ^ b) * 2 + (x ^ a), 0, False)
+            back = [(target, source) for source, target in output_pairs(a, b)]
+            output_grad = output_grad + lax.ppermute(piece, AXES, back).astype(F32)
+    triple_grad = scatter_columns(
+        member_array, x, zh, contract_rows(normed, grad_mixed).astype(BF16), triple_columns
+    )
+    first_gain_grad = jnp.sum(triple_grad * triple_weight.astype(F32), axis=-1) / first_gain.astype(F32)
+    second_gain_grad = jnp.sum(up_grad * up_weight.astype(F32), axis=-1) / second_gain.astype(F32)
+    return (
+        layer_output,
+        token_grad,
+        triple_grad,
+        output_grad,
+        up_grad,
+        down_grad,
+        first_gain_grad,
+        second_gain_grad,
+    )
+
+
 def solution(mesh):
+    grouped = mesh.shape["dp"] * 2 == mesh.shape["fsdp"] == MEMBERS
+    rows = P(AXES, None)
     return jax.shard_map(
-        body,
+        grouped_body if grouped else whole_rows_body,
         mesh=mesh,
-        in_specs=(
-            P(("dp", "fsdp"), None),
-            P(("dp", "fsdp"), None),
-            P(("dp", "fsdp"), None),
-            P(("dp", "fsdp"), None),
-            P(("dp", "fsdp"), None),
-            P(("dp", "fsdp")),
-            P(("dp", "fsdp")),
-            P(("dp", "fsdp"), None),
-            P("dp", None),
-            P("dp", None, None),
-            P("dp", None, None),
-        ),
-        out_specs=(
-            P(("dp", "fsdp"), None),
-            P(("dp", "fsdp"), None),
-            P(("dp", "fsdp"), None),
-            P(("dp", "fsdp"), None),
-            P(("dp", "fsdp"), None),
-            P(("dp", "fsdp"), None),
-            P(("dp", "fsdp")),
-            P(("dp", "fsdp")),
-        ),
+        in_specs=(rows,) * 5 + (P(AXES),) * 2 + (rows, P("dp", None), P("dp", None, None), P("dp", None, None)),
+        out_specs=(rows,) * 6 + (P(AXES),) * 2,
         check_vma=False,
     )

time: 4580 us -> 671 us (0.15)
  waiting for transfers between devices: 4060 us -> 363 us
  blocking collectives: 193 us -> 0 us
  matrix products: 244 us -> 56.5 us
  starting transfers between devices: 1.1 us -> 155 us
    reduce_scatter x4 -> x0, waiting for transfers between devices: 3390 us -> none  [the longest x1 1410 us: body(): lax.psum_scatter(down_term, ('dp', 'fsdp'), scatter_dimension=0, tiled=True)]
    all_gather x8 -> x0, waiting for transfers between devices: 676 us -> none  [the longest x1 191 us: body(): lax.all_gather(down_weight, ('dp', 'fsdp'), axis=0, tiled=True)]
    ppermute x0 -> x105, waiting for transfers between devices: none -> 363 us  [the longest x93 349 us: swap(): return lax.ppermute(array, AXES, [(i, i ^ bits) for i in range(DEVICES)])]
    dot_general x19 -> x16, matrix products: 244 us -> 56.5 us  [the longest x4 17.8 us: contract_rows(): lax.dot_general(left, right, (((0,), (0,)), ((), ())), preferred_element_...]
    ppermute x0 -> x105, starting transfers between devices: none -> 155 us  [the longest x93 132 us: swap(): return lax.ppermute(array, AXES, [(i, i ^ bits) for i in range(DEVICES)])]
    unnamed x2 -> x0, blocking collectives: 109 us -> none
    all_gather x3 -> x0, blocking collectives: 84.7 us -> none  [the longest x1 32 us: body(): lax.all_gather(delta_rows.T, 'fsdp', axis=0, tiled=True)]
  transfers between devices with their start and end apart: 12 -> 105, of which waited for: 10 -> 39; matrix products, arithmetic and copies ran while one was open for 6% -> 10% of each run, Pallas kernels for 0% -> 6%
where the time goes in v1:
time: 671 us; the launch traced here: 666 us
  waiting for transfers between devices  363 us (54%)
  starting transfers between devices  155 us (23%)
  matrix products  56.5 us (8%)
  Pallas kernels  42.1 us (6%)
  other arithmetic  32.7 us (5%)
  local copies, waits for them, and re-layouts  12.4 us (2%)
    ppermute x93, waiting for transfers between devices, swap(): return lax.ppermute(array, AXES, [(i, i ^ bits) for i in range(DEVICES)])  349 us
    ppermute x93, starting transfers between devices, swap(): return lax.ppermute(array, AXES, [(i, i ^ bits) for i in range(DEVICES)])  132 us
    dot_general x4, matrix products, contract_rows(): lax.dot_general(left, right, (((0,), (0,)), ((), ())), preferred_element_...  17.8 us
    pallas_call x4, Pallas kernels, place_rows(): pl.pallas_call(kernel, out_shape=jax.ShapeDtypeStruct((total * rows, widt...  14.4 us
  transfers between devices with their start and end apart: 105, of which 39 were waited for; matrix products, arithmetic and copies ran while one was open for 10% of the time, Pallas kernels for 6%

profile of v1, /device:TPU:1, one launch (start us, length us, event | category | flops | bytes accessed | tf_op | source)
XLA Modules:
  0.0 665.7 jit_solution(7490563605689758783)
XLA Ops:
  25.6 9.1 %collective-permute-done.10 = bf16[2,2,64]{2,1,0:T(2,128)(2,1)S(1)} collective-permute-done((bf16[2,2,64]{2,1,0:T(2,128)(2,1)S(1)}, bf16[2,2,64]{2,1,0:T(2,128)(2,1)S(1)}, u32[]{:S(2)}, u32[]{:S(2)}) %collective-permute-start.10) | collective-permute-done | bytes 544 | tf_op jit(solution)/shard_map/ppermute | solution.py:427
  48.9 3.2 collective-permute-start.19
  55.7 4.2 collective-permute-start.27
  61.7 6.0 collective-permute-start.57
  67.6 4.6 collective-permute-done.27.rest_3_
  75.2 8.8 %collective-permute-done.2 = bf16[128,2048]{1,0:T(8,128)(2,1)S(1)} collective-permute-done((bf16[128,2048]{1,0:T(8,128)(2,1)}, bf16[128,2048]{1,0:T(8,128)(2,1)S(1)}, u32[]{:S(2)}, u32[]{:S(2)}) %collective-permute-start.2) | collective-permute-done | bytes 524320 | tf_op jit(solution)/shard_map/ppermute | solution.py:427
  85.4 3.5 collective-permute-start.6
  88.9 22.4 %collective-permute-done.4 = bf16[128,2048]{1,0:T(8,128)(2,1)S(1)} collective-permute-done((bf16[128,2048]{1,0:T(8,128)(2,1)}, bf16[128,2048]{1,0:T(8,128)(2,1)S(1)}, u32[]{:S(2)}, u32[]{:S(2)}) %collective-permute-start.4) | collective-permute-done | bytes 524320 | tf_op jit(solution)/shard_map/ppermute | solution.py:427
  118.8 13.3 %collective-permute-done.22.rest_2_ = bf16[512,768]{1,0:T(8,128)(2,1)S(1)} collective-permute-done((bf16[512,768]{1,0:T(8,128)(2,1)S(1)}, bf16[512,768]{1,0:T(8,128)(2,1)S(1)}, u32[]{:S(2)}, u32[]{:S(2)}) %collective-permute-start.22) | collective-permute-done | bytes 786464 | tf_op jit(solution)/shard_map/ppermute | solution.py:427
  134.7 14.3 %collective-permute-done.23.rest_3_ = bf16[512,768]{1,0:T(8,128)(2,1)S(1)} collective-permute-done((bf16[512,768]{1,0:T(8,128)(2,1)S(1)}, bf16[512,768]{1,0:T(8,128)(2,1)S(1)}, u32[]{:S(2)}, u32[]{:S(2)}) %collective-permute-start.23) | collective-permute-done | bytes 786464 | tf_op jit(solution)/shard_map/ppermute | solution.py:427
  149.0 3.2 collective-permute-start.42
  152.2 5.7 shard_map.180
  157.9 5.4 fusion.40.mixed_ref
  163.3 9.0 %shard_map.181 = (bf16[1024,256]{1,0:T(8,128)(2,1)S(1)}, bf16[1024,256]{1,0:T(8,128)(2,1)S(1)}, bf16[1024,256]{1,0:T(8,128)(2,1)S(1)}, bf16[1024,256]{1,0:T(8,128)(2,1)S(1)}) custom-call(s32[3]{0:T(128)S(1)} %pad_add_fusion.1.layout_ref, f32[1024,768]{1,0:T(8,128)} %fusion.40.mixed_ref, f32[1024,128]{1,0:T(8,128)S(1)} %get-tuple-element.128.cos_ref, ...), custom_call_target="tpu_custom_call" | custom-call | tf_op jit(solution)/shard_map/pallas_call | solution.py:684
  182.9 3.1 collective-permute-start.58
  187.4 10.0 %collective-permute-done.58 = bf16[128,2048]{1,0:T(8,128)(2,1)S(1)} collective-permute-done((bf16[128,2048]{1,0:T(8,128)(2,1)S(1)}, bf16[128,2048]{1,0:T(8,128)(2,1)S(1)}, u32[]{:S(2)}, u32[]{:S(2)}) %collective-permute-start.58) | collective-permute-done | bytes 524320 | tf_op jit(solution)/shard_map/ppermute | solution.py:427
  198.2 15.9 %collective-permute-done.59 = bf16[128,2048]{1,0:T(8,128)(2,1)S(1)} collective-permute-done((bf16[128,2048]{1,0:T(8,128)(2,1)S(1)}, bf16[128,2048]{1,0:T(8,128)(2,1)S(1)}, u32[]{:S(2)}, u32[]{:S(2)}) %collective-permute-start.59) | collective-permute-done | bytes 524320 | tf_op jit(solution)/shard_map/ppermute | solution.py:427
  217.0 3.3 collective-permute-start.29
  220.2 12.0 %collective-permute-done.60 = bf16[128,2048]{1,0:T(8,128)(2,1)S(1)} collective-permute-done((bf16[128,2048]{1,0:T(8,128)(2,1)S(1)}, bf16[128,2048]{1,0:T(8,128)(2,1)S(1)}, u32[]{:S(2)}, u32[]{:S(2)}) %collective-permute-start.60) | collective-permute-done | bytes 524320 | tf_op jit(solution)/shard_map/ppermute | solution.py:427
  235.7 23.8 %collective-permute-done.29 = bf16[128,2048]{1,0:T(8,128)(2,1)S(1)} collective-permute-done((bf16[128,2048]{1,0:T(8,128)(2,1)S(1)}, bf16[128,2048]{1,0:T(8,128)(2,1)S(1)}, u32[]{:S(2)}, u32[]{:S(2)}) %collective-permute-start.29) | collective-permute-done | bytes 524320 | tf_op jit(solution)/shard_map/ppermute | solution.py:427
  259.5 9.6 %collective-permute-done.31 = bf16[128,2048]{1,0:T(8,128)(2,1)S(1)} collective-permute-done((bf16[128,2048]{1,0:T(8,128)(2,1)S(1)}, bf16[128,2048]{1,0:T(8,128)(2,1)S(1)}, u32[]{:S(2)}, u32[]{:S(2)}) %collective-permute-start.31) | collective-permute-done | bytes 524320 | tf_op jit(solution)/shard_map/ppermute | solution.py:427
  271.7 8.2 %collective-permute-done.46.rest_1_ = bf16[512,1024]{1,0:T(8,128)(2,1)S(1)} collective-permute-done((bf16[512,1024]{1,0:T(8,128)(2,1)S(1)}, bf16[512,1024]{1,0:T(8,128)(2,1)S(1)}, u32[]{:S(2)}, u32[]{:S(2)}) %collective-permute-start.46) | collective-permute-done | bytes 1048608 | tf_op jit(solution)/shard_map/ppermute | solution.py:427
  282.4 24.5 %collective-permute-done.51.rest_3_ = bf16[256,2048]{1,0:T(8,128)(2,1)S(1)} collective-permute-done((bf16[256,2048]{1,0:T(8,128)(2,1)S(1)}, bf16[256,2048]{1,0:T(8,128)(2,1)S(1)}, u32[]{:S(2)}, u32[]{:S(2)}) %collective-permute-start.51) | collective-permute-done | bytes 1048608 | tf_op jit(solution)/shard_map/ppermute | solution.py:427
  308.3 21.1 %collective-permute-done.48.rest_3_ = bf16[512,1024]{1,0:T(8,128)(2,1)S(1)} collective-permute-done((bf16[512,1024]{1,0:T(8,128)(2,1)S(1)}, bf16[512,1024]{1,0:T(8,128)(2,1)S(1)}, u32[]{:S(2)}, u32[]{:S(2)}) %collective-permute-start.48) | collective-permute-done | bytes 1048608 | tf_op jit(solution)/shard_map/ppermute | solution.py:427
  329.4 7.2 %shard_map.184 = bf16[2048,1024]{1,0:T(8,128)(2,1)S(1)} custom-call(s32[32]{0:T(128)S(1)} %broadcast_xor_fusion.places_ref, bf16[512,1024]{1,0:T(8,128)(2,1)S(1)} %constant_dynamic-update-slice_fusion.24.rest_0_, bf16[512,1024]{1,0:T(8,128)(2,1)S(1)} %collective-permute-done.46.rest_1_, bf16[512,1024]{1,0:T(8,128)(2,1)S(1)} %collective-permute-done.47.rest_2_, ...), custom_call_target="tpu_custom_call" | custom-call | tf_op jit(solution)/shard_map/pallas_call | solution.py:531
  341.3 6.0 fusion.47
  347.3 8.8 %fusion.11 = (bf16[1024,1024]{1,0:T(8,128)(2,1)S(1)}, bf16[1024,1024]{1,0:T(8,128)(2,1)S(1)}) fusion(f32[1024,1024]{1,0:T(8,128)} %fusion.47, bf16[1024,2048]{1,0:T(8,128)(2,1)S(1)} %constant_dynamic-update-slice_fusion.32, bf16[1024,2048]{1,0:T(8,128)(2,1)S(1)} %shard_map.185), kind=kOutput, calls=%fused_computation.15 | convolution fusion | flops 4318035968 | bytes 16777216 | tf_op jit(solution)/shard_map/dot_general | solution.py:763
  356.1 5.3 convolution_convert_fusion.1
  361.4 3.7 convolution_convert_fusion.3
  365.1 3.7 convolution_convert_fusion.5
  375.7 6.6 convolution_convert_fusion
  387.9 29.4 %collective-permute-done.94 = bf16[2,2,256,1024]{3,2,0,1:T(8,128)(2,1)S(1)} collective-permute-done((bf16[2,2,256,1024]{3,2,0,1:T(8,128)(2,1)}, bf16[2,2,256,1024]{3,2,0,1:T(8,128)(2,1)S(1)}, u32[]{:S(2)}, u32[]{:S(2)}) %collective-permute-start.94) | collective-permute-done | bytes 2097184 | tf_op jit(solution)/shard_map/ppermute | solution.py:427
  421.0 26.9 %collective-permute-done.66 = bf16[128,2048]{1,0:T(8,128)(2,1)S(1)} collective-permute-done((bf16[128,2048]{1,0:T(8,128)(2,1)S(1)}, bf16[128,2048]{1,0:T(8,128)(2,1)S(1)}, u32[]{:S(2)}, u32[]{:S(2)}) %collective-permute-start.66) | collective-permute-done | bytes 524320 | tf_op jit(solution)/shard_map/ppermute | solution.py:427
  447.9 8.2 %collective-permute-done.68 = bf16[128,2048]{1,0:T(8,128)(2,1)S(1)} collective-permute-done((bf16[128,2048]{1,0:T(8,128)(2,1)S(1)}, bf16[128,2048]{1,0:T(8,128)(2,1)S(1)}, u32[]{:S(2)}, u32[]{:S(2)}) %collective-permute-start.68) | collective-permute-done | bytes 524320 | tf_op jit(solution)/shard_map/ppermute | solution.py:427
  458.3 3.4 collective-permute-start.69
  466.9 28.6 %collective-permute-start.72 = (bf16[128,2048]{1,0:T(8,128)(2,1)S(1)}, bf16[128,2048]{1,0:T(8,128)(2,1)S(1)}, u32[]{:S(2)}, u32[]{:S(2)}) collective-permute-start(bf16[128,2048]{1,0:T(8,128)(2,1)S(1)} %get-tuple-element.86), channel_id=1, source_target_pairs={{0,8},{1,9},{2,10},{3,11},{4,12},{5,13},{6,14},{7,15},{8,0},{9,1},... | collective-permute-start | bytes 1572872 | tf_op jit(solution)/shard_map/ppermute | solution.py:427
  497.8 9.0 %collective-permute-done.70 = bf16[128,2048]{1,0:T(8,128)(2,1)S(1)} collective-permute-done((bf16[128,2048]{1,0:T(8,128)(2,1)S(1)}, bf16[128,2048]{1,0:T(8,128)(2,1)S(1)}, u32[]{:S(2)}, u32[]{:S(2)}) %collective-permute-start.70) | collective-permute-done | bytes 524320 | tf_op jit(solution)/shard_map/ppermute | solution.py:427
  506.8 6.0 collective-permute-start.73
  521.2 11.0 %shard_map.186 = bf16[1024,768]{1,0:T(8,128)(2,1)S(1)} custom-call(s32[3]{0:T(128)S(1)} %pad_add_fusion.1.layout_ref, bf16[1024,256]{1,0:T(8,128)(2,1)S(1)} %get-tuple-element.61.q_ref, bf16[1024,256]{1,0:T(8,128)(2,1)S(1)} %get-tuple-element.62.k_ref, bf16[1024,256]{1,0:T(8,128)(2,1)S(1)} %get-tuple-element.63.v_ref, ...), custom_call_target="tpu_custom_call" | custom-call | tf_op jit(solution)/shard_map/pallas_call | solution.py:732
  532.2 4.6 convolution_convert_fusion.2
  543.3 3.1 fusion.13
  557.1 20.9 %collective-permute-done.81 = bf16[2,2,256,768]{3,2,0,1:T(8,128)(2,1)S(1)} collective-permute-done((bf16[2,2,256,768]{3,2,0,1:T(8,128)(2,1)S(1)}, bf16[2,2,256,768]{3,2,0,1:T(8,128)(2,1)S(1)}, u32[]{:S(2)}, u32[]{:S(2)}) %collective-permute-start.81) | collective-permute-done | bytes 1572896 | tf_op jit(solution)/shard_map/ppermute | solution.py:427
  582.9 31.9 %collective-permute-done.82.came_ref = bf16[512,768]{1,0:T(8,128)(2,1)S(1)} collective-permute-done((bf16[512,768]{1,0:T(8,128)(2,1)S(1)}, bf16[512,768]{1,0:T(8,128)(2,1)S(1)}, u32[]{:S(2)}, u32[]{:S(2)}) %collective-permute-start.82) | collective-permute-done | bytes 786464 | tf_op jit(solution)/shard_map/ppermute | solution.py:427
  616.8 10.1 %collective-permute-done.79 = bf16[128,2048]{1,0:T(8,128)(2,1)S(1)} collective-permute-done((bf16[128,2048]{1,0:T(8,128)(2,1)S(1)}, bf16[128,2048]{1,0:T(8,128)(2,1)S(1)}, u32[]{:S(2)}, u32[]{:S(2)}) %collective-permute-start.79) | collective-permute-done | bytes 524320 | tf_op jit(solution)/shard_map/ppermute | solution.py:427
  628.7 5.2 collective-permute-start.84
  636.6 4.0 collective-permute-start.86
  640.6 3.8 collective-permute-start.87
  654.2 8.6 %collective-permute-done.80 = bf16[128,2048]{1,0:T(8,128)(2,1)S(1)} collective-permute-done((bf16[128,2048]{1,0:T(8,128)(2,1)S(1)}, bf16[128,2048]{1,0:T(8,128)(2,1)S(1)}, u32[]{:S(2)}, u32[]{:S(2)}) %collective-permute-start.80) | collective-permute-done | bytes 524320 | tf_op jit(solution)/shard_map/ppermute | solution.py:443
  (362 shorter events, 162.0 us)
Async XLA Ops:
  6.4 55.0 %collective-permute-start.25 = (bf16[64,2048]{1,0:T(8,128)(2,1)}, bf16[64,2048]{1,0:T(8,128)(2,1)S(1)}, u32[]{:S(2)}, u32[]{:S(2)}) collective-permute-start(bf16[64,2048]{1,0:T(8,128)(2,1)} %param.14), channel_id=1, source_target_pairs={{0,4},{1,20},{2,6},{3,22},{4,0},{5,16},{6,2},{7,18},{8,12},{9,28},... | collective-permute-start | bytes 786440 | tf_op jit(solution)/shard_map/ppermute | solution.py:803
  8.7 51.5 %collective-permute-start = (bf16[128,2048]{1,0:T(8,128)(2,1)}, bf16[128,2048]{1,0:T(8,128)(2,1)}, u32[]{:S(2)}, u32[]{:S(2)}) collective-permute-start(bf16[128,2048]{1,0:T(8,128)(2,1)} %param.12), channel_id=1, source_target_pairs={{0,0},{1,1},{2,2},{3,3},{4,8},{5,9},{6,10},{7,11},{8,4},{9,5},{10,... | collective-permute-start | bytes 1572872 | tf_op jit(solution)/shard_map/ppermute | solution.py:443
  13.3 33.1 %collective-permute-start.14 = (bf16[64,768]{1,0:T(8,128)(2,1)}, bf16[64,768]{1,0:T(8,128)(2,1)S(1)}, u32[]{:S(2)}, u32[]{:S(2)}) collective-permute-start(bf16[64,768]{1,0:T(8,128)(2,1)} %get-tuple-element.45), channel_id=1, source_target_pairs={{0,1},{1,0},{2,3},{3,2},{4,5},{5,4},{6,7},{7,6},{8,9},{9,8},{10,11... | collective-permute-start | bytes 294920 | tf_op jit(solution)/shard_map/ppermute | solution.py:427
  20.3 28.5 %collective-permute-start.15 = (bf16[64,768]{1,0:T(8,128)(2,1)}, bf16[64,768]{1,0:T(8,128)(2,1)S(1)}, u32[]{:S(2)}, u32[]{:S(2)}) collective-permute-start(bf16[64,768]{1,0:T(8,128)(2,1)} %get-tuple-element.46), channel_id=1, source_target_pairs={{0,2},{1,3},{2,0},{3,1},{4,6},{5,7},{6,4},{7,5},{8,10},{9,11},{10,... | collective-permute-start | bytes 294920 | tf_op jit(solution)/shard_map/ppermute | solution.py:427
  61.7 121.2 %collective-permute-start.57 = (bf16[128,2048]{1,0:T(8,128)(2,1)}, bf16[128,2048]{1,0:T(8,128)(2,1)S(1)}, u32[]{:S(2)}, u32[]{:S(2)}) collective-permute-start(bf16[128,2048]{1,0:T(8,128)(2,1)} %param.19), channel_id=1, source_target_pairs={{0,0},{1,1},{2,2},{3,3},{4,8},{5,9},{6,10},{7,11},{8,4},{9,5},{10,... | collective-permute-start | bytes 1572872 | tf_op jit(solution)/shard_map/ppermute | solution.py:443
  72.3 43.0 %collective-permute-start.21 = (bf16[512,768]{1,0:T(8,128)(2,1)S(1)}, bf16[512,768]{1,0:T(8,128)(2,1)S(1)}, u32[]{:S(2)}, u32[]{:S(2)}) collective-permute-start(bf16[512,768]{1,0:T(8,128)(2,1)S(1)} %constant_dynamic-update-slice_fusion.8.rest_0_), channel_id=1, source_target_pairs={{0,4},{1,5},{2,6},{3,7},{4,0},{5,1},{6,2},{7,3},{8,12},{9,13},{10,... | collective-permute-start | bytes 2359304 | tf_op jit(solution)/shard_map/ppermute | solution.py:427
  73.4 38.0 %collective-permute-start.4 = (bf16[128,2048]{1,0:T(8,128)(2,1)}, bf16[128,2048]{1,0:T(8,128)(2,1)S(1)}, u32[]{:S(2)}, u32[]{:S(2)}) collective-permute-start(bf16[128,2048]{1,0:T(8,128)(2,1)} %collective-permute-done), channel_id=1, source_target_pairs={{0,3},{1,2},{2,1},{3,0},{4,7},{5,6},{6,5},{7,4},{8,11},{9,10},{10,... | collective-permute-start | bytes 1572872 | tf_op jit(solution)/shard_map/ppermute | solution.py:427
  112.1 61.0 %collective-permute-start.39 = (bf16[64,1024]{1,0:T(8,128)(2,1)S(1)}, bf16[64,1024]{1,0:T(8,128)(2,1)S(1)}, u32[]{:S(2)}, u32[]{:S(2)}) collective-permute-start(bf16[64,1024]{1,0:T(8,128)(2,1)S(1)} %copy-done.23), channel_id=1, source_target_pairs={{0,1},{1,0},{2,3},{3,2},{4,5},{5,4},{6,7},{7,6},{8,9},{9,8},{10,11... | collective-permute-start | bytes 393224 | tf_op jit(solution)/shard_map/ppermute | solution.py:427
  113.3 59.9 %collective-permute-start.40 = (bf16[64,1024]{1,0:T(8,128)(2,1)S(1)}, bf16[64,1024]{1,0:T(8,128)(2,1)S(1)}, u32[]{:S(2)}, u32[]{:S(2)}) collective-permute-start(bf16[64,1024]{1,0:T(8,128)(2,1)S(1)} %copy-done.22), channel_id=1, source_target_pairs={{0,2},{1,3},{2,0},{3,1},{4,6},{5,7},{6,4},{7,5},{8,10},{9,11},{10,... | collective-permute-start | bytes 393224 | tf_op jit(solution)/shard_map/ppermute | solution.py:427
  116.4 32.6 %collective-permute-start.23 = (bf16[512,768]{1,0:T(8,128)(2,1)S(1)}, bf16[512,768]{1,0:T(8,128)(2,1)S(1)}, u32[]{:S(2)}, u32[]{:S(2)}) collective-permute-start(bf16[512,768]{1,0:T(8,128)(2,1)S(1)} %collective-permute-done.21.rest_1_), channel_id=1, source_target_pairs={{0,16},{1,17},{2,18},{3,19},{4,20},{5,21},{6,22},{7,23},{8,24},{9,... | collective-permute-start | bytes 2359304 | tf_op jit(solution)/shard_map/ppermute | solution.py:427
  132.2 42.5 %collective-permute-start.41 = (bf16[64,1024]{1,0:T(8,128)(2,1)S(1)}, bf16[64,1024]{1,0:T(8,128)(2,1)S(1)}, u32[]{:S(2)}, u32[]{:S(2)}) collective-permute-start(bf16[64,1024]{1,0:T(8,128)(2,1)S(1)} %copy-done.21), channel_id=1, source_target_pairs={{0,3},{1,2},{2,1},{3,0},{4,7},{5,6},{6,5},{7,4},{8,11},{9,10},{10,... | collective-permute-start | bytes 393224 | tf_op jit(solution)/shard_map/ppermute | solution.py:427
  173.1 43.2 %collective-permute-start.28 = (bf16[512,2048]{1,0:T(8,128)(2,1)S(1)}, bf16[512,2048]{1,0:T(8,128)(2,1)S(1)}, u32[]{:S(2)}, u32[]{:S(2)}) collective-permute-start(bf16[512,2048]{1,0:T(8,128)(2,1)S(1)} %convolution_convert_fusion.7), channel_id=1, source_target_pairs={{0,8},{1,9},{2,10},{3,11},{4,12},{5,13},{6,14},{7,15},{8,0},{9,1},... | collective-permute-start | bytes 6291464 | tf_op jit(solution)/shard_map/ppermute | solution.py:427
  179.1 54.6 %collective-permute-start.49 = (bf16[256,2048]{1,0:T(8,128)(2,1)S(1)}, bf16[256,2048]{1,0:T(8,128)(2,1)S(1)}, u32[]{:S(2)}, u32[]{:S(2)}) collective-permute-start(bf16[256,2048]{1,0:T(8,128)(2,1)S(1)} %copy-done.2), channel_id=1, source_target_pairs={{0,4},{1,5},{2,6},{3,7},{4,0},{5,1},{6,2},{7,3},{8,12},{9,13},{10,... | collective-permute-start | bytes 3145736 | tf_op jit(solution)/shard_map/ppermute | solution.py:427
  187.3 32.9 %collective-permute-start.61 = (bf16[128,2048]{1,0:T(8,128)(2,1)S(1)}, bf16[128,2048]{1,0:T(8,128)(2,1)S(1)}, u32[]{:S(2)}, u32[]{:S(2)}) collective-permute-start(bf16[128,2048]{1,0:T(8,128)(2,1)S(1)} %collective-permute-done.57), channel_id=1, source_target_pairs={{0,8},{1,9},{2,10},{3,11},{4,12},{5,13},{6,14},{7,15},{8,0},{9,1},... | collective-permute-start | bytes 1572872 | tf_op jit(solution)/shard_map/ppermute | solution.py:427
  197.4 34.8 %collective-permute-start.60 = (bf16[128,2048]{1,0:T(8,128)(2,1)S(1)}, bf16[128,2048]{1,0:T(8,128)(2,1)S(1)}, u32[]{:S(2)}, u32[]{:S(2)}) collective-permute-start(bf16[128,2048]{1,0:T(8,128)(2,1)S(1)} %collective-permute-done.57), channel_id=1, source_target_pairs={{0,3},{1,2},{2,1},{3,0},{4,7},{5,6},{6,5},{7,4},{8,11},{9,10},{10,... | collective-permute-start | bytes 1572872 | tf_op jit(solution)/shard_map/ppermute | solution.py:427
  217.0 42.5 %collective-permute-start.29 = (bf16[128,2048]{1,0:T(8,128)(2,1)S(1)}, bf16[128,2048]{1,0:T(8,128)(2,1)S(1)}, u32[]{:S(2)}, u32[]{:S(2)}) collective-permute-start(bf16[128,2048]{1,0:T(8,128)(2,1)S(1)} %get-tuple-element.106), channel_id=1, source_target_pairs={{0,3},{1,2},{2,1},{3,0},{4,7},{5,6},{6,5},{7,4},{8,11},{9,10},{10,... | collective-permute-start | bytes 1572872 | tf_op jit(solution)/shard_map/ppermute | solution.py:427
  220.2 48.9 %collective-permute-start.31 = (bf16[128,2048]{1,0:T(8,128)(2,1)S(1)}, bf16[128,2048]{1,0:T(8,128)(2,1)S(1)}, u32[]{:S(2)}, u32[]{:S(2)}) collective-permute-start(bf16[128,2048]{1,0:T(8,128)(2,1)S(1)} %get-tuple-element.107), channel_id=1, source_target_pairs={{0,2},{1,3},{2,0},{3,1},{4,6},{5,7},{6,4},{7,5},{8,10},{9,11},{10,... | collective-permute-start | bytes 1572872 | tf_op jit(solution)/shard_map/ppermute | solution.py:427
  232.3 36.9 %collective-permute-start.30 = (bf16[128,2048]{1,0:T(8,128)(2,1)S(1)}, bf16[128,2048]{1,0:T(8,128)(2,1)S(1)}, u32[]{:S(2)}, u32[]{:S(2)}) collective-permute-start(bf16[128,2048]{1,0:T(8,128)(2,1)S(1)} %get-tuple-element.108), channel_id=1, source_target_pairs={{0,1},{1,0},{2,3},{3,2},{4,5},{5,4},{6,7},{7,6},{8,9},{9,8},{10,11... | collective-permute-start | bytes 1572872 | tf_op jit(solution)/shard_map/ppermute | solution.py:427
  233.7 37.5 %collective-permute-start.50 = (bf16[256,2048]{1,0:T(8,128)(2,1)S(1)}, bf16[256,2048]{1,0:T(8,128)(2,1)S(1)}, u32[]{:S(2)}, u32[]{:S(2)}) collective-permute-start(bf16[256,2048]{1,0:T(8,128)(2,1)S(1)} %copy-done.2), channel_id=1, source_target_pairs={{0,16},{1,17},{2,18},{3,19},{4,20},{5,21},{6,22},{7,23},{8,24},{9,... | collective-permute-start | bytes 3145736 | tf_op jit(solution)/shard_map/ppermute | solution.py:427
  233.8 46.0 %collective-permute-start.46 = (bf16[512,1024]{1,0:T(8,128)(2,1)S(1)}, bf16[512,1024]{1,0:T(8,128)(2,1)S(1)}, u32[]{:S(2)}, u32[]{:S(2)}) collective-permute-start(bf16[512,1024]{1,0:T(8,128)(2,1)S(1)} %constant_dynamic-update-slice_fusion.24.rest_0_), channel_id=1, source_target_pairs={{0,4},{1,5},{2,6},{3,7},{4,0},{5,1},{6,2},{7,3},{8,12},{9,13},{10,... | collective-permute-start | bytes 3145736 | tf_op jit(solution)/shard_map/ppermute | solution.py:427
  259.5 48.8 %collective-permute-start.47 = (bf16[512,1024]{1,0:T(8,128)(2,1)S(1)}, bf16[512,1024]{1,0:T(8,128)(2,1)S(1)}, u32[]{:S(2)}, u32[]{:S(2)}) collective-permute-start(bf16[512,1024]{1,0:T(8,128)(2,1)S(1)} %constant_dynamic-update-slice_fusion.24.rest_0_), channel_id=1, source_target_pairs={{0,16},{1,17},{2,18},{3,19},{4,20},{5,21},{6,22},{7,23},{8,24},{9,... | collective-permute-start | bytes 3145736 | tf_op jit(solution)/shard_map/ppermute | solution.py:427
  269.1 37.8 %collective-permute-start.51 = (bf16[256,2048]{1,0:T(8,128)(2,1)S(1)}, bf16[256,2048]{1,0:T(8,128)(2,1)S(1)}, u32[]{:S(2)}, u32[]{:S(2)}) collective-permute-start(bf16[256,2048]{1,0:T(8,128)(2,1)S(1)} %collective-permute-done.49.rest_1_), channel_id=1, source_target_pairs={{0,16},{1,17},{2,18},{3,19},{4,20},{5,21},{6,22},{7,23},{8,24},{9,... | collective-permute-start | bytes 3145736 | tf_op jit(solution)/shard_map/ppermute | solution.py:427
  279.8 49.6 %collective-permute-start.48 = (bf16[512,1024]{1,0:T(8,128)(2,1)S(1)}, bf16[512,1024]{1,0:T(8,128)(2,1)S(1)}, u32[]{:S(2)}, u32[]{:S(2)}) collective-permute-start(bf16[512,1024]{1,0:T(8,128)(2,1)S(1)} %collective-permute-done.46.rest_1_), channel_id=1, source_target_pairs={{0,16},{1,17},{2,18},{3,19},{4,20},{5,21},{6,22},{7,23},{8,24},{9,... | collective-permute-start | bytes 3145736 | tf_op jit(solution)/shard_map/ppermute | solution.py:427
  281.2 56.1 %collective-permute-start.34 = (bf16[128,2048]{1,0:T(8,128)(2,1)S(1)}, bf16[128,2048]{1,0:T(8,128)(2,1)S(1)}, u32[]{:S(2)}, u32[]{:S(2)}) collective-permute-start(bf16[128,2048]{1,0:T(8,128)(2,1)S(1)} %get-tuple-element.90), channel_id=1, source_target_pairs={{0,3},{1,2},{2,1},{3,0},{4,7},{5,6},{6,5},{7,4},{8,11},{9,10},{10,... | collective-permute-start | bytes 1572872 | tf_op jit(solution)/shard_map/ppermute | solution.py:427
  282.2 55.2 %collective-permute-start.33 = (bf16[128,2048]{1,0:T(8,128)(2,1)S(1)}, bf16[128,2048]{1,0:T(8,128)(2,1)S(1)}, u32[]{:S(2)}, u32[]{:S(2)}) collective-permute-start(bf16[128,2048]{1,0:T(8,128)(2,1)S(1)} %get-tuple-element.90), channel_id=1, source_target_pairs={{0,2},{1,3},{2,0},{3,1},{4,6},{5,7},{6,4},{7,5},{8,10},{9,11},{10,... | collective-permute-start | bytes 1572872 | tf_op jit(solution)/shard_map/ppermute | solution.py:427
  306.9 30.9 %collective-permute-start.32 = (bf16[128,2048]{1,0:T(8,128)(2,1)S(1)}, bf16[128,2048]{1,0:T(8,128)(2,1)S(1)}, u32[]{:S(2)}, u32[]{:S(2)}) collective-permute-start(bf16[128,2048]{1,0:T(8,128)(2,1)S(1)} %get-tuple-element.90), channel_id=1, source_target_pairs={{0,1},{1,0},{2,3},{3,2},{4,5},{5,4},{6,7},{7,6},{8,9},{9,8},{10,11... | collective-permute-start | bytes 1572872 | tf_op jit(solution)/shard_map/ppermute | solution.py:427
  370.3 47.1 %collective-permute-start.94 = (bf16[2,2,256,1024]{3,2,0,1:T(8,128)(2,1)}, bf16[2,2,256,1024]{3,2,0,1:T(8,128)(2,1)S(1)}, u32[]{:S(2)}, u32[]{:S(2)}) collective-permute-start(bf16[2,2,256,1024]{3,2,0,1:T(8,128)(2,1)} %copy_bitcast_fusion), channel_id=1, source_target_pairs={{0,16},{1,17},{2,18},{3,19},{4,20},{5,21},{6,22},{7,23},{8,24},{9,... | collective-permute-start | bytes 6291464 | tf_op jit(solution)/shard_map/ppermute | solution.py:427
  382.9 34.4 %collective-permute-start.53 = (bf16[128,2048]{1,0:T(8,128)(2,1)S(1)}, bf16[128,2048]{1,0:T(8,128)(2,1)S(1)}, u32[]{:S(2)}, u32[]{:S(2)}) collective-permute-start(bf16[128,2048]{1,0:T(8,128)(2,1)S(1)} %get-tuple-element.103), channel_id=1, source_target_pairs={{0,3},{1,2},{2,1},{3,0},{4,7},{5,6},{6,5},{7,4},{8,11},{9,10},{10,... | collective-permute-start | bytes 1572872 | tf_op jit(solution)/shard_map/ppermute | solution.py:427
  383.0 35.0 %collective-permute-start.55 = (bf16[128,2048]{1,0:T(8,128)(2,1)S(1)}, bf16[128,2048]{1,0:T(8,128)(2,1)S(1)}, u32[]{:S(2)}, u32[]{:S(2)}) collective-permute-start(bf16[128,2048]{1,0:T(8,128)(2,1)S(1)} %get-tuple-element.104), channel_id=1, source_target_pairs={{0,2},{1,3},{2,0},{3,1},{4,6},{5,7},{6,4},{7,5},{8,10},{9,11},{10,... | collective-permute-start | bytes 1572872 | tf_op jit(solution)/shard_map/ppermute | solution.py:427
  384.5 77.8 %collective-permute-start.103 = (bf16[2,256,2048]{2,1,0:T(8,128)(2,1)S(1)}, bf16[2,256,2048]{2,1,0:T(8,128)(2,1)S(1)}, u32[]{:S(2)}, u32[]{:S(2)}) collective-permute-start(bf16[2,256,2048]{2,1,0:T(8,128)(2,1)S(1)} %dynamic-slice_bitcast_fusion), channel_id=1, source_target_pairs={{0,16},{1,17},{2,18},{3,19},{4,20},{5,21},{6,22},{7,23},{8,24},{9,... | collective-permute-start | bytes 6291464 | tf_op jit(solution)/shard_map/ppermute | solution.py:427
  385.3 35.6 %collective-permute-start.54 = (bf16[128,2048]{1,0:T(8,128)(2,1)S(1)}, bf16[128,2048]{1,0:T(8,128)(2,1)S(1)}, u32[]{:S(2)}, u32[]{:S(2)}) collective-permute-start(bf16[128,2048]{1,0:T(8,128)(2,1)S(1)} %get-tuple-element.105), channel_id=1, source_target_pairs={{0,1},{1,0},{2,3},{3,2},{4,5},{5,4},{6,7},{7,6},{8,9},{9,8},{10,11... | collective-permute-start | bytes 1572872 | tf_op jit(solution)/shard_map/ppermute | solution.py:427
  417.3 30.6 %collective-permute-start.66 = (bf16[128,2048]{1,0:T(8,128)(2,1)S(1)}, bf16[128,2048]{1,0:T(8,128)(2,1)S(1)}, u32[]{:S(2)}, u32[]{:S(2)}) collective-permute-start(bf16[128,2048]{1,0:T(8,128)(2,1)S(1)} %get-tuple-element.98), channel_id=1, source_target_pairs={{0,3},{1,2},{2,1},{3,0},{4,7},{5,6},{6,5},{7,4},{8,11},{9,10},{10,... | collective-permute-start | bytes 1572872 | tf_op jit(solution)/shard_map/ppermute | solution.py:427
  417.3 38.7 %collective-permute-start.68 = (bf16[128,2048]{1,0:T(8,128)(2,1)S(1)}, bf16[128,2048]{1,0:T(8,128)(2,1)S(1)}, u32[]{:S(2)}, u32[]{:S(2)}) collective-permute-start(bf16[128,2048]{1,0:T(8,128)(2,1)S(1)} %get-tuple-element.99), channel_id=1, source_target_pairs={{0,2},{1,3},{2,0},{3,1},{4,6},{5,7},{6,4},{7,5},{8,10},{9,11},{10,... | collective-permute-start | bytes 1572872 | tf_op jit(solution)/shard_map/ppermute | solution.py:427
  418.0 38.0 %collective-permute-start.67 = (bf16[128,2048]{1,0:T(8,128)(2,1)S(1)}, bf16[128,2048]{1,0:T(8,128)(2,1)S(1)}, u32[]{:S(2)}, u32[]{:S(2)}) collective-permute-start(bf16[128,2048]{1,0:T(8,128)(2,1)S(1)} %get-tuple-element.100), channel_id=1, source_target_pairs={{0,1},{1,0},{2,3},{3,2},{4,5},{5,4},{6,7},{7,6},{8,9},{9,8},{10,11... | collective-permute-start | bytes 1572872 | tf_op jit(solution)/shard_map/ppermute | solution.py:427
  420.9 46.0 %collective-permute-start.95 = (bf16[512,1024]{1,0:T(8,128)(2,1)S(1)}, bf16[512,1024]{1,0:T(8,128)(2,1)S(1)}, u32[]{:S(2)}, u32[]{:S(2)}) collective-permute-start(bf16[512,1024]{1,0:T(8,128)(2,1)S(1)} %fusion.14), channel_id=1, source_target_pairs={{0,4},{1,5},{2,6},{3,7},{4,0},{5,1},{6,2},{7,3},{8,12},{9,13},{10,... | collective-permute-start | bytes 3145736 | tf_op jit(solution)/shard_map/ppermute | solution.py:427
  458.3 37.5 %collective-permute-start.69 = (bf16[128,2048]{1,0:T(8,128)(2,1)S(1)}, bf16[128,2048]{1,0:T(8,128)(2,1)S(1)}, u32[]{:S(2)}, u32[]{:S(2)}) collective-permute-start(bf16[128,2048]{1,0:T(8,128)(2,1)S(1)} %get-tuple-element.86), channel_id=1, source_target_pairs={{0,1},{1,0},{2,3},{3,2},{4,5},{5,4},{6,7},{7,6},{8,9},{9,8},{10,11... | collective-permute-start | bytes 1572872 | tf_op jit(solution)/shard_map/ppermute | solution.py:427
  463.9 74.8 %collective-permute-start.104 = (bf16[256,2048]{1,0:T(8,128)(2,1)}, bf16[256,2048]{1,0:T(8,128)(2,1)}, u32[]{:S(2)}, u32[]{:S(2)}) collective-permute-start(bf16[256,2048]{1,0:T(8,128)(2,1)} %fusion.12), channel_id=1, source_target_pairs={{0,4},{1,5},{2,6},{3,7},{4,0},{5,1},{6,2},{7,3},{8,12},{9,13},{10,... | collective-permute-start | bytes 3145736 | tf_op jit(solution)/shard_map/ppermute | solution.py:427
  463.9 49.0 %collective-permute-start.71 = (bf16[128,2048]{1,0:T(8,128)(2,1)S(1)}, bf16[128,2048]{1,0:T(8,128)(2,1)S(1)}, u32[]{:S(2)}, u32[]{:S(2)}) collective-permute-start(bf16[128,2048]{1,0:T(8,128)(2,1)S(1)} %get-tuple-element.86), channel_id=1, source_target_pairs={{0,3},{1,2},{2,1},{3,0},{4,7},{5,6},{6,5},{7,4},{8,11},{9,10},{10,... | collective-permute-start | bytes 1572872 | tf_op jit(solution)/shard_map/ppermute | solution.py:427
  466.4 40.4 %collective-permute-start.70 = (bf16[128,2048]{1,0:T(8,128)(2,1)S(1)}, bf16[128,2048]{1,0:T(8,128)(2,1)S(1)}, u32[]{:S(2)}, u32[]{:S(2)}) collective-permute-start(bf16[128,2048]{1,0:T(8,128)(2,1)S(1)} %get-tuple-element.86), channel_id=1, source_target_pairs={{0,2},{1,3},{2,0},{3,1},{4,6},{5,7},{6,4},{7,5},{8,10},{9,11},{10,... | collective-permute-start | bytes 1572872 | tf_op jit(solution)/shard_map/ppermute | solution.py:427
  466.9 46.1 %collective-permute-start.72 = (bf16[128,2048]{1,0:T(8,128)(2,1)S(1)}, bf16[128,2048]{1,0:T(8,128)(2,1)S(1)}, u32[]{:S(2)}, u32[]{:S(2)}) collective-permute-start(bf16[128,2048]{1,0:T(8,128)(2,1)S(1)} %get-tuple-element.86), channel_id=1, source_target_pairs={{0,8},{1,9},{2,10},{3,11},{4,12},{5,13},{6,14},{7,15},{8,0},{9,1},... | collective-permute-start | bytes 1572872 | tf_op jit(solution)/shard_map/ppermute | solution.py:427
  495.8 43.7 %collective-permute-start.56 = (bf16[128,2048]{1,0:T(8,128)(2,1)}, bf16[128,2048]{1,0:T(8,128)(2,1)}, u32[]{:S(2)}, u32[]{:S(2)}) collective-permute-start(bf16[128,2048]{1,0:T(8,128)(2,1)} %get-tuple-element.119), channel_id=1, source_target_pairs={{0,0},{1,1},{2,2},{3,3},{4,8},{5,9},{6,10},{7,11},{8,4},{9,5},{10,... | collective-permute-start | bytes 1572872 | tf_op jit(solution)/shard_map/ppermute | solution.py:443
  542.5 35.5 %collective-permute-start.81 = (bf16[2,2,256,768]{3,2,0,1:T(8,128)(2,1)S(1)}, bf16[2,2,256,768]{3,2,0,1:T(8,128)(2,1)S(1)}, u32[]{:S(2)}, u32[]{:S(2)}) collective-permute-start(bf16[2,2,256,768]{3,2,0,1:T(8,128)(2,1)S(1)} %copy_bitcast_fusion.1), channel_id=1, source_target_pairs={{0,16},{1,17},{2,18},{3,19},{4,20},{5,21},{6,22},{7,23},{8,24},{9,... | collective-permute-start | bytes 4718600 | tf_op jit(solution)/shard_map/ppermute | solution.py:427
  542.5 35.9 %collective-permute-start.76 = (bf16[512,2048]{1,0:T(8,128)(2,1)S(1)}, bf16[512,2048]{1,0:T(8,128)(2,1)S(1)}, u32[]{:S(2)}, u32[]{:S(2)}) collective-permute-start(bf16[512,2048]{1,0:T(8,128)(2,1)S(1)} %convolution_convert_fusion.9), channel_id=1, source_target_pairs={{0,8},{1,9},{2,10},{3,11},{4,12},{5,13},{6,14},{7,15},{8,0},{9,1},... | collective-permute-start | bytes 6291464 | tf_op jit(solution)/shard_map/ppermute | solution.py:427
  578.3 36.4 %collective-permute-start.82 = (bf16[512,768]{1,0:T(8,128)(2,1)S(1)}, bf16[512,768]{1,0:T(8,128)(2,1)S(1)}, u32[]{:S(2)}, u32[]{:S(2)}) collective-permute-start(bf16[512,768]{1,0:T(8,128)(2,1)S(1)} %fusion.16), channel_id=1, source_target_pairs={{0,4},{1,5},{2,6},{3,7},{4,0},{5,1},{6,2},{7,3},{8,12},{9,13},{10,... | collective-permute-start | bytes 2359304 | tf_op jit(solution)/shard_map/ppermute | solution.py:427
  579.1 36.6 %collective-permute-start.77 = (bf16[128,2048]{1,0:T(8,128)(2,1)S(1)}, bf16[128,2048]{1,0:T(8,128)(2,1)S(1)}, u32[]{:S(2)}, u32[]{:S(2)}) collective-permute-start(bf16[128,2048]{1,0:T(8,128)(2,1)S(1)} %get-tuple-element.95), channel_id=1, source_target_pairs={{0,3},{1,2},{2,1},{3,0},{4,7},{5,6},{6,5},{7,4},{8,11},{9,10},{10,... | collective-permute-start | bytes 1572872 | tf_op jit(solution)/shard_map/ppermute | solution.py:427
  581.1 45.8 %collective-permute-start.79 = (bf16[128,2048]{1,0:T(8,128)(2,1)S(1)}, bf16[128,2048]{1,0:T(8,128)(2,1)S(1)}, u32[]{:S(2)}, u32[]{:S(2)}) collective-permute-start(bf16[128,2048]{1,0:T(8,128)(2,1)S(1)} %get-tuple-element.96), channel_id=1, source_target_pairs={{0,2},{1,3},{2,0},{3,1},{4,6},{5,7},{6,4},{7,5},{8,10},{9,11},{10,... | collective-permute-start | bytes 1572872 | tf_op jit(solution)/shard_map/ppermute | solution.py:427
  581.8 45.2 %collective-permute-start.78 = (bf16[128,2048]{1,0:T(8,128)(2,1)S(1)}, bf16[128,2048]{1,0:T(8,128)(2,1)S(1)}, u32[]{:S(2)}, u32[]{:S(2)}) collective-permute-start(bf16[128,2048]{1,0:T(8,128)(2,1)S(1)} %get-tuple-element.97), channel_id=1, source_target_pairs={{0,1},{1,0},{2,3},{3,2},{4,5},{5,4},{6,7},{7,6},{8,9},{9,8},{10,11... | collective-permute-start | bytes 1572872 | tf_op jit(solution)/shard_map/ppermute | solution.py:427
  581.9 46.8 %collective-permute-start.90 = (bf16[64,2048]{1,0:T(8,128)(2,1)S(1)}, bf16[64,2048]{1,0:T(8,128)(2,1)S(1)}, u32[]{:S(2)}, u32[]{:S(2)}) collective-permute-start(bf16[64,2048]{1,0:T(8,128)(2,1)S(1)} %get-tuple-element.115), channel_id=1, source_target_pairs={{0,0},{16,1},{2,2},{18,3},{4,4},{20,5},{6,6},{22,7},{8,8},{24,9},{... | collective-permute-start | bytes 786440 | tf_op jit(solution)/shard_map/ppermute | solution.py:868
  (84 other events, 1240.1 us)

commit v2 on v0

--- a/solution.py
+++ b/solution.py
@@ -3,6 +3,8 @@
 import jax
 import jax.numpy as jnp
 from jax import lax
+from jax.experimental import pallas as pl
+from jax.experimental.pallas import tpu as pltpu
 from jax.sharding import PartitionSpec as P
 
 HEADS = 16
@@ -200,7 +202,7 @@
     return (result, attended_low, middle, normed_two, hidden, activation)
 
 
-def body(
+def whole_rows_body(
     tokens,
     triple_weight,
     output_weight,
@@ -408,32 +410,724 @@
     )
 
 
+AXES = ("dp", "fsdp")
+DEVICES = 32
+MEMBERS = 8
+CORE, ZL, Y = 8, 2, 1
+X, ZH = 16, 4
+BF16 = jnp.bfloat16
+F32 = jnp.float32
+SMEM = pl.BlockSpec(memory_space=pltpu.SMEM)
+VMEM = pl.BlockSpec(memory_space=pltpu.VMEM)
+HBM = pl.BlockSpec(memory_space=pltpu.HBM)
+
+
+def swap(array, bits):
+    return lax.ppermute(array, AXES, [(i, i ^ bits) for i in range(DEVICES)])
+
+
+def alike(*bits):
+    groups = {}
+    for i in range(DEVICES):
+        groups.setdefault(i & ~sum(bits), []).append(i)
+    return list(groups.values())
+
+
+def exchange(array, *bits):
+    return lax.all_to_all(array, AXES, 0, 0, tiled=True, axis_index_groups=alike(*bits))
+
+
+def after(array, *others):
+    return lax.optimization_barrier((array,) + others)[0]
+
+
+def together(*arrays):
+    return lax.optimization_barrier(arrays)
+
+
+def regroup_pairs():
+    def target(i):
+        x, core, zh, low = i >> 4, (i >> 3) & 1, (i >> 2) & 1, i & 3
+        return (x << 4) | (zh << 3) | (core << 2) | low
+
+    return [(i, target(i)) for i in range(DEVICES)]
+
+
+def regroup(array):
+    return lax.ppermute(array, AXES, regroup_pairs())
+
+
+def turn_pairs():
+    return [(i, (i & 14) | (i & 1) << 4 | i >> 4) for i in range(DEVICES)]
+
+
+def gather(own, *bits):
+    return lax.all_gather(own, AXES, axis=0, tiled=True, axis_index_groups=alike(*bits))
+
+
+def collect(parts):
+    return exchange(parts.reshape(4, -1, parts.shape[1]), ZL, Y)
+
+
+def row_product(half, left, right, transposed, came=None):
+    count, depth = left.shape[0] // 2, left.shape[1]
+    width = right.shape[0] if transposed else right.shape[1]
+    tile = 512
+
+    def kernel(half_ref, left_ref, right_ref, *rest):
+        if transposed:
+            total = dot_transposed(left_ref[...], right_ref[...])
+        else:
+            total = jnp.dot(left_ref[...], right_ref[...], preferred_element_type=F32)
+        if came is not None:
+            total = total + rest[0][...].astype(F32)
+        rest[-1][...] = total.astype(BF16)
+
+    columns = pl.BlockSpec((count, tile), lambda i, half_ref: (0, i))
+    if transposed:
+        right_spec = pl.BlockSpec((tile, depth), lambda i, half_ref: (i, 0))
+    else:
+        right_spec = pl.BlockSpec((depth, tile), lambda i, half_ref: (0, i))
+    more = [] if came is None else [came]
+    return pl.pallas_call(
+        kernel,
+        grid_spec=pltpu.PrefetchScalarGridSpec(
+            num_scalar_prefetch=1,
+            grid=(width // tile,),
+            in_specs=[pl.BlockSpec((count, depth), lambda i, half_ref: (half_ref[0], 0)), right_spec]
+            + [columns] * len(more),
+            out_specs=columns,
+        ),
+        out_shape=jax.ShapeDtypeStruct((count, width), BF16),
+        compiler_params=pltpu.CompilerParams(vmem_limit_bytes=32 << 20),
+    )(half, left, right, *more)
+
+
+def product_sums(core, rows, right, transposed=False):
+    near, far = core.reshape(1), (1 - core).reshape(1)
+    came = swap(row_product(far, rows, right, transposed), CORE)
+    return row_product(near, rows, right, transposed, came)
+
+
+def hidden_columns(member, width):
+    core, zl, y = (member >> 2) & 1, (member >> 1) & 1, member & 1
+    return [
+        ((gx * X + core * CORE + gz * ZH + zl * ZL + y) * width, width)
+        for gx in range(2)
+        for gz in range(2)
+    ]
+
+
+def head_columns(member, width):
+    core, zl, y = (member >> 2) & 1, (member >> 1) & 1, member & 1
+    return [
+        (part * width + ((y * 2 + core) * 4 + half * 2 + zl) * HEAD, HEAD)
+        for part in range(3)
+        for half in range(2)
+    ]
+
+
+def deal_columns(own, columns, extra=None):
+    rows = own.shape[0]
+    width = own.shape[1] // MEMBERS
+    more = 0 if extra is None else 16
+
+    def kernel(*refs):
+        own_ref, slabs_ref = refs[0], refs[-1]
+        for member in range(MEMBERS):
+            start = 0
+            for place, size in columns(member):
+                slabs_ref[member, :rows, start : start + size] = own_ref[:, place : place + size]
+                start += size
+            if more:
+                slabs_ref[member, rows:, :] = jnp.zeros((more, width), own.dtype)
+                slabs_ref[member, rows:, : extra.shape[1]] = jnp.broadcast_to(refs[1][...], (more, extra.shape[1]))
+
+    arrays = [own] if extra is None else [own, extra]
+    return pl.pallas_call(
+        kernel,
+        out_shape=jax.ShapeDtypeStruct((MEMBERS, rows + more, width), own.dtype),
+        in_specs=[VMEM] * len(arrays),
+        out_specs=VMEM,
+    )(*arrays)
+
+
+def pair_up(index, mine, theirs):
+    return jnp.where(index == 0, jnp.stack([mine, theirs]), jnp.stack([theirs, mine]))
+
+
+def row_copies(places_ref, pieces, whole_ref, sems, rows):
+    sources = [(piece, start) for piece in pieces for start in range(0, piece.shape[0], rows)]
+    return [
+        pltpu.make_async_copy(
+            piece.at[pl.ds(start, rows)],
+            whole_ref.at[pl.ds(pl.multiple_of(places_ref[n] * rows, rows), rows)],
+            sems.at[n],
+        )
+        for n, (piece, start) in enumerate(sources)
+    ]
+
+
+def place_rows(places, pieces, rows):
+    count = sum(piece.shape[0] for piece in pieces)
+
+    def kernel(places_ref, *rest):
+        whole_ref, sems = rest[-2:]
+        copies = row_copies(places_ref, rest[:-2], whole_ref, sems, rows)
+        for copy in copies:
+            copy.start()
+        for copy in copies:
+            copy.wait()
+
+    return pl.pallas_call(
+        kernel,
+        out_shape=jax.ShapeDtypeStruct((count, pieces[0].shape[1]), BF16),
+        in_specs=[SMEM] + [HBM] * len(pieces),
+        out_specs=VMEM,
+        scratch_shapes=[pltpu.SemaphoreType.DMA((count // rows,))],
+        compiler_params=pltpu.CompilerParams(vmem_limit_bytes=16 << 20),
+    )(places, *pieces)
+
+
+def place_columns(slabs, own, gain, columns):
+    rows = own.shape[0]
+
+    def kernel(slabs_ref, own_ref, gain_ref, whole_ref, sum_ref):
+        total = jnp.zeros((rows, HEAD), F32)
+        for member in range(MEMBERS):
+            start = 0
+            for place, size in columns(member):
+                part = slabs_ref[member, :, start : start + size].astype(F32)
+                whole_ref[:, place : place + size] = part
+                product = part * own_ref[:, place : place + size].astype(F32)
+                for lane in range(0, size, HEAD):
+                    total = total + product[:, lane : lane + HEAD]
+                start += size
+        sum_ref[...] = jnp.sum(total, axis=1, keepdims=True) / gain_ref[...]
+
+    return pl.pallas_call(
+        kernel,
+        out_shape=[jax.ShapeDtypeStruct(own.shape, F32), jax.ShapeDtypeStruct((rows, 1), F32)],
+        in_specs=[VMEM] * 3,
+        out_specs=[VMEM] * 2,
+        compiler_params=pltpu.CompilerParams(vmem_limit_bytes=32 << 20),
+    )(slabs, own, gain)
+
+
+def give(index, bits, grad):
+    return swap(lax.dynamic_index_in_dim(grad, 1 - index, 0, False), bits)
+
+
+def half_sum(first, second, grad, came):
+    outer, inner, width = grad.shape[1], grad.shape[3], grad.shape[4]
+    mine = lax.dynamic_slice(grad, (first, 0, second, 0, 0), (1, outer, 1, inner, width))
+    theirs = lax.dynamic_slice(came, (0, second, 0, 0), (outer, 1, inner, width))
+    shape = (outer, inner, width)
+    return mine.reshape(shape).astype(F32) + theirs.reshape(shape).astype(F32)
+
+
+def give_sum(first, second, bits, grad, came):
+    return swap(half_sum(first, 1 - second, grad, came).astype(BF16), bits)
+
+
+def keep_sum(first, second, grad, came, far):
+    return half_sum(first, second, grad, came) + far.astype(F32)
+
+
+def turn(vectors, cosine, sine):
+    return vectors * cosine + pltpu.roll(vectors, HEAD // 2, 1) * sine
+
+
+def block_mask(ends_ref, block, block_rows, count):
+    first_end, second_end = ends_ref[0], ends_ref[1]
+    place = lax.broadcasted_iota(jnp.int32, (block_rows, 1), 0) + block * block_rows
+    key_place = lax.broadcasted_iota(jnp.int32, (1, count), 1)
+    start = jnp.where(place < first_end, 0, jnp.where(place < second_end, first_end, second_end))
+    return (key_place <= place) & (key_place >= start)
+
+
+def masked_probs(queries, keys, allowed):
+    scores = lax.dot_general(queries, keys, (((1,), (1,)), ((), ())), preferred_element_type=F32)
+    scores = jnp.where(allowed, scores * HEAD ** (-0.5), MASKED)
+    weights = jnp.exp(scores - jnp.max(scores, axis=-1, keepdims=True))
+    return weights * (1.0 / jnp.sum(weights, axis=-1, keepdims=True))
+
+
+BLOCK = 256
+
+
+def attention_forward(ends, places, normal, pieces, cosine, sine):
+    count, depth = normal.shape
+    width = pieces[0].shape[1] // 3
+    block_rows = depth // 8
+
+    def kernel(ends_ref, places_ref, normal_ref, cos_ref, sin_ref, *rest):
+        piece_refs, (q_ref, k_ref, v_ref, out_ref, weight_ref, sems) = rest[: len(pieces)], rest[len(pieces) :]
+        copies = row_copies(places_ref, piece_refs, weight_ref, sems, block_rows)
+        for copy in copies:
+            copy.start()
+        for copy in copies:
+            copy.wait()
+
+        @pl.loop(0, count // BLOCK)
+        def _(block):
+            here = pl.ds(pl.multiple_of(block * BLOCK, BLOCK), BLOCK)
+            mixed = jnp.dot(normal_ref[here, :], weight_ref[...], preferred_element_type=F32)
+            cos, sin = cos_ref[here, :], sin_ref[here, :]
+            v_ref[here, :] = mixed[:, 2 * width :].astype(BF16)
+            for head in range(width // HEAD):
+                span = slice(head * HEAD, (head + 1) * HEAD)
+                key_span = slice(width + head * HEAD, width + (head + 1) * HEAD)
+                q_ref[here, span] = turn(mixed[:, span], cos, sin).astype(BF16)
+                k_ref[here, span] = turn(mixed[:, key_span], cos, sin).astype(BF16)
+
+        @pl.loop(0, count // BLOCK)
+        def _(block):
+            here = pl.ds(pl.multiple_of(block * BLOCK, BLOCK), BLOCK)
+            allowed = block_mask(ends_ref, block, BLOCK, count)
+            for head in range(width // HEAD):
+                span = slice(head * HEAD, (head + 1) * HEAD)
+                probs = masked_probs(q_ref[here, span], k_ref[:, span], allowed)
+                out_ref[here, span] = jnp.dot(
+                    probs.astype(BF16), v_ref[:, span], preferred_element_type=F32
+                ).astype(BF16)
+
+    return pl.pallas_call(
+        kernel,
+        out_shape=[jax.ShapeDtypeStruct((count, width), BF16)] * 4
+        + [jax.ShapeDtypeStruct((depth, 3 * width), BF16)],
+        in_specs=[SMEM] * 2 + [VMEM] * 3 + [HBM] * len(pieces),
+        out_specs=[VMEM] * 5,
+        scratch_shapes=[pltpu.SemaphoreType.DMA((8,))],
+        compiler_params=pltpu.CompilerParams(vmem_limit_bytes=48 << 20),
+    )(ends, places, normal, cosine, sine, *pieces)
+
+
+def attention_backward_heads(ends, queries, keys, values, grad_out, cosine, sine):
+    count, width = queries.shape
+
+    def kernel(ends_ref, q_ref, k_ref, v_ref, g_ref, cos_ref, sin_ref, out_ref, gk_ref, gv_ref):
+        gk_ref[...] = jnp.zeros_like(gk_ref)
+        gv_ref[...] = jnp.zeros_like(gv_ref)
+
+        @pl.loop(0, count // BLOCK)
+        def _(block):
+            here = pl.ds(pl.multiple_of(block * BLOCK, BLOCK), BLOCK)
+            allowed = block_mask(ends_ref, block, BLOCK, count)
+            for head in range(width // HEAD):
+                span = slice(head * HEAD, (head + 1) * HEAD)
+                q, g = q_ref[here, span], g_ref[here, span]
+                probs = masked_probs(q, k_ref[:, span], allowed)
+                grad_probs = lax.dot_general(
+                    g, v_ref[:, span], (((1,), (1,)), ((), ())), preferred_element_type=F32
+                )
+                delta = jnp.sum(probs * grad_probs, axis=-1, keepdims=True)
+                grad_scores = (probs * (grad_probs - delta)).astype(BF16)
+                grad_query = jnp.dot(grad_scores, k_ref[:, span], preferred_element_type=F32)
+                out_ref[here, span] = turn(
+                    grad_query * HEAD ** (-0.5), cos_ref[here, :], -sin_ref[here, :]
+                ).astype(BF16)
+                over_rows = (((0,), (0,)), ((), ()))
+                gk_ref[:, span] += lax.dot_general(grad_scores, q, over_rows, preferred_element_type=F32)
+                gv_ref[:, span] += lax.dot_general(
+                    probs.astype(BF16), g, over_rows, preferred_element_type=F32
+                )
+
+        out_ref[:, 2 * width :] = gv_ref[...].astype(BF16)
+        for head in range(width // HEAD):
+            span = slice(head * HEAD, (head + 1) * HEAD)
+            out_ref[:, width + head * HEAD : width + (head + 1) * HEAD] = turn(
+                gk_ref[:, span] * HEAD ** (-0.5), cos_ref[...], -sin_ref[...]
+            ).astype(BF16)
+
+    return pl.pallas_call(
+        kernel,
+        out_shape=jax.ShapeDtypeStruct((count, 3 * width), BF16),
+        in_specs=[SMEM] + [VMEM] * 6,
+        out_specs=VMEM,
+        scratch_shapes=[pltpu.VMEM((count, width), F32), pltpu.VMEM((count, width), F32)],
+        compiler_params=pltpu.CompilerParams(vmem_limit_bytes=48 << 20),
+    )(ends, queries, keys, values, grad_out, cosine, sine)
+
+
+def norm_parts(values):
+    centred = values - jnp.mean(values, axis=-1, keepdims=True)
+    inverse = lax.rsqrt(jnp.mean(centred * centred, axis=-1, keepdims=True) + EPSILON)
+    return centred * inverse, inverse
+
+
+def norm_backward(values, scaled):
+    normal, inverse = norm_parts(values)
+    return inverse * (
+        scaled
+        - jnp.mean(scaled, axis=-1, keepdims=True)
+        - normal * jnp.mean(scaled * normal, axis=-1, keepdims=True)
+    )
+
+
+ROWS = 64
+
+
+def norm_of(values, gain):
+    def kernel(values_ref, gain_ref, out_ref):
+        out_ref[...] = (norm_parts(values_ref[...].astype(F32))[0] * gain_ref[...]).astype(BF16)
+
+    count, width = values.shape
+    return pl.pallas_call(
+        kernel,
+        grid=(count // ROWS,),
+        out_shape=jax.ShapeDtypeStruct(values.shape, BF16),
+        in_specs=[pl.BlockSpec((ROWS, width), lambda i: (i, 0)), pl.BlockSpec((1, width), lambda i: (0, 0))],
+        out_specs=pl.BlockSpec((ROWS, width), lambda i: (i, 0)),
+    )(values, gain)
+
+
+def row_kernel(kernel, parts, arrays, gain, outs):
+    rows, width = parts.shape[1:]
+    whole = pl.BlockSpec((4, ROWS, width), lambda i: (0, i, 0))
+    single = pl.BlockSpec((ROWS, width), lambda i: (i, 0))
+    return pl.pallas_call(
+        kernel,
+        grid=(rows // ROWS,),
+        out_shape=[jax.ShapeDtypeStruct((rows, width), kind) for kind in outs],
+        in_specs=[whole] + [single] * len(arrays) + [pl.BlockSpec((1, width), lambda i: (0, 0))],
+        out_specs=[single] * len(outs),
+    )(parts, *arrays, gain)
+
+
+def add_parts(parts_ref):
+    total = parts_ref[0].astype(F32)
+    for i in range(1, 4):
+        total = total + parts_ref[i].astype(F32)
+    return total
+
+
+def middle_rows(parts, inputs, gain):
+    def kernel(parts_ref, inputs_ref, gain_ref, middle_ref, normal_ref):
+        middle = inputs_ref[...].astype(F32) + add_parts(parts_ref)
+        middle_ref[...] = middle
+        normal_ref[...] = (norm_parts(middle)[0] * gain_ref[...]).astype(BF16)
+
+    return row_kernel(kernel, parts, [inputs], gain, [F32, BF16])
+
+
+def grad_middle_rows(parts, middle, cotangent, gain):
+    def kernel(parts_ref, middle_ref, cotangent_ref, gain_ref, grad_ref, branch_ref):
+        grad = cotangent_ref[...].astype(F32) + norm_backward(middle_ref[...], add_parts(parts_ref) * gain_ref[...])
+        grad_ref[...] = grad
+        branch_ref[...] = grad.astype(BF16)
+
+    return row_kernel(kernel, parts, [middle, cotangent], gain, [F32, BF16])
+
+
+def token_grad_rows(parts, inputs, grad_middle, gain):
+    def kernel(parts_ref, inputs_ref, middle_ref, gain_ref, grad_ref):
+        grad = norm_backward(inputs_ref[...].astype(F32), add_parts(parts_ref) * gain_ref[...])
+        grad_ref[...] = (middle_ref[...] + grad).astype(BF16)
+
+    return row_kernel(kernel, parts, [inputs, grad_middle], gain, [BF16])[0]
+
+
+def feed_forward(normal, grad_activation, places, pieces, piece_rows):
+    count, width = normal.shape
+    hidden_width = pieces[0].shape[1]
+    step_rows = 256
+    steps = count // step_rows
+
+    def kernel(places_ref, normal_ref, grad_activation_ref, *rest):
+        act_ref, grad_ref, up_out, up_ref, sems, out_sem = rest[len(pieces) :]
+        step = pl.program_id(0)
+        copies = row_copies(places_ref, rest[: len(pieces)], up_ref, sems, piece_rows)
+        back = pltpu.make_async_copy(up_ref, up_out, out_sem)
+
+        @pl.when(step == 0)
+        def _():
+            for copy in copies:
+                copy.start()
+            for copy in copies:
+                copy.wait()
+            back.start()
+
+        hidden = jnp.dot(normal_ref[...], up_ref[...], preferred_element_type=F32)
+        scale = math.sqrt(2.0 / math.pi)
+        square = hidden * hidden
+        tanh = jnp.tanh(scale * hidden * (1.0 + 0.044715 * square))
+        act_ref[...] = (0.5 * hidden * (1.0 + tanh)).astype(BF16)
+        slope = 0.5 * (1.0 + tanh) + (0.5 * scale) * hidden * (1.0 - tanh * tanh) * (
+            1.0 + (3.0 * 0.044715) * square
+        )
+        grad_ref[...] = (grad_activation_ref[...] * slope).astype(BF16)
+
+        @pl.when(step == steps - 1)
+        def _():
+            back.wait()
+
+    row_spec = pl.BlockSpec((step_rows, width), lambda i: (i, 0))
+    hidden_spec = pl.BlockSpec((step_rows, hidden_width), lambda i: (i, 0))
+    return pl.pallas_call(
+        kernel,
+        grid=(steps,),
+        out_shape=[jax.ShapeDtypeStruct((count, hidden_width), BF16)] * 2
+        + [jax.ShapeDtypeStruct((width, hidden_width), BF16)],
+        in_specs=[SMEM, row_spec, hidden_spec] + [HBM] * len(pieces),
+        out_specs=[hidden_spec, hidden_spec, HBM],
+        scratch_shapes=[
+            pltpu.VMEM((width, hidden_width), BF16),
+            pltpu.SemaphoreType.DMA((width // piece_rows,)),
+            pltpu.SemaphoreType.DMA,
+        ],
+        compiler_params=pltpu.CompilerParams(vmem_limit_bytes=48 << 20),
+    )(places, normal, grad_activation, *pieces)
+
+
+def contract_rows(left, right):
+    return lax.dot_general(left, right, (((0,), (0,)), ((), ())), preferred_element_type=F32)
+
+
+def dot_transposed(left, right):
+    return lax.dot_general(left, right, (((1,), (1,)), ((), ())), preferred_element_type=F32)
+
+
+def grouped_body(
+    tokens,
+    triple_weight,
+    output_weight,
+    up_weight,
+    down_weight,
+    first_gain,
+    second_gain,
+    cotangent,
+    frame_counts,
+    text_counts,
+    action_counts,
+):
+    rows, width = tokens.shape
+    count = rows * MEMBERS
+    dp, fsdp = lax.axis_index("dp"), lax.axis_index("fsdp")
+    x, core = dp >> 1, dp & 1
+    zh = fsdp >> 2
+
+    counts = jnp.concatenate(
+        [frame_counts.reshape(-1), text_counts.reshape(-1), action_counts.reshape(-1)]
+    )
+    counts = jnp.where(core == zh, counts, swap(counts, CORE))
+    frames = counts[:2]
+    slots = text_counts.shape[-1]
+    texts = counts[2 : 2 + 2 * slots].reshape(2, slots)
+    actions = counts[2 + 2 * slots :].reshape(2, slots)
+    live = jnp.arange(slots, dtype=jnp.int32) < frames[:, None]
+    lengths = jnp.sum(jnp.where(live, IMG + texts + actions, 0), axis=-1)
+    first_end = lengths[0]
+    second_end = lengths[0] + lengths[1]
+    ends = jnp.stack([first_end, second_end]).astype(jnp.int32)
+    places = jnp.arange(count, dtype=jnp.int32)
+    starts = jnp.where(places < first_end, 0, jnp.where(places < second_end, first_end, second_end))
+    cosine, sine = rotary_tables(places - starts)
+    cosine = jnp.concatenate([cosine[:, 0], cosine[:, 0]], axis=1)
+    sine = jnp.concatenate([-sine[:, 0], sine[:, 0]], axis=1)
+
+    hidden_width = up_weight.shape[1] // DEVICES
+    triple_columns = lambda m: head_columns(m, width)
+    up_columns = lambda m: hidden_columns(m, hidden_width)
+    first_column = first_gain.astype(F32)[:, None]
+    second_column = second_gain.astype(F32)[:, None]
+    sides = ((0, 0), (0, 1), (1, 0), (1, 1))
+    rows_of_weight = triple_weight.shape[0]
+    block = rows_of_weight * 4
+    half_block = down_weight.shape[0] // 4
+
+    def places_of(pieces):
+        return jnp.stack([place for a, b, parts in pieces for place in parts(x ^ a, zh ^ b)]).astype(jnp.int32)
+
+    def column_places(*which):
+        return lambda sx, sz: [sx * 4 + c * 2 + sz for c in which]
+
+    def down_places(*which):
+        return lambda sx, sz: [(sx * 2 + sz) * 4 + q for q in which]
+
+    triple_own = deal_columns(triple_weight, triple_columns, jnp.concatenate([first_gain, second_gain])[None])
+    triple_own = exchange(triple_own, CORE, ZL, Y)
+    inputs = regroup(tokens)
+    down_x = swap(down_weight, X)
+    turned = lax.ppermute(output_weight, AXES, turn_pairs())
+    cotangent = regroup(cotangent)
+    quarters = [down_weight[q * half_block : (q + 1) * half_block] for q in range(4)]
+    up_dealt = deal_columns(up_weight, up_columns)
+    gains = triple_own[:, rows_of_weight, : 2 * rows_of_weight]
+    triple_own = triple_own[:, :rows_of_weight].reshape(-1, triple_own.shape[-1])
+    triple_own, inputs, down_x, turned, gains, cotangent, ends, quarters, up_dealt = together(
+        triple_own, inputs, down_x, turned, gains, cotangent, ends, quarters, up_dealt
+    )
+    all_inputs = gather(inputs, CORE, ZL, Y)
+    triple_zh = swap(triple_own, ZH)
+    triple_x = swap(triple_own, X)
+    gains = pair_up(zh, gains, swap(gains, ZH))
+    gains = pair_up(x, gains, swap(gains, X))
+    gains = gains.reshape(2, 2, 2, 4, 2, -1).transpose(4, 0, 2, 1, 3, 5).reshape(2, -1).astype(F32)
+    all_inputs, triple_zh, triple_x, gains, cosine, sine, turned, cotangent, up_dealt, quarters = together(
+        all_inputs, triple_zh, triple_x, gains, cosine, sine, turned, cotangent, up_dealt, quarters
+    )
+    triple_xz = swap(triple_zh, X)
+    all_cotangent = gather(cotangent, CORE, ZL, Y)
+    turned_zh = swap(turned, ZH)
+    down_zh = [swap(quarters[0], ZH)]
+    normal = norm_of(all_inputs, gains[:1])
+    pair = pair_up(zh, turned, turned_zh)
+    triple_xz, normal, pair, down_zh, quarters, up_dealt = together(
+        triple_xz, normal, pair, down_zh, quarters, up_dealt
+    )
+    up_own = exchange(up_dealt, CORE, ZL, Y)
+    up_own = up_own.reshape(-1, up_own.shape[-1])
+    up_halves = [up_own[:block], up_own[block:]]
+    pair_x = swap(pair, X)
+    down_zh += [swap(quarters[1], ZH), swap(quarters[2], ZH)]
+    down_xz = [swap(down_zh[0], X)]
+    queries, keys, values, attended, triple = attention_forward(
+        ends,
+        places_of([(a, b, column_places(0, 1)) for a, b in sides]),
+        normal,
+        [triple_own, triple_zh, triple_x, triple_xz],
+        cosine,
+        sine,
+    )
+    output = jnp.where(x == 0, jnp.stack([pair, pair_x], axis=1), jnp.stack([pair_x, pair], axis=1))
+    output = output.reshape(-1, width)
+    down_zh, down_xz, attended, output, up_own, up_halves, quarters = together(
+        down_zh, down_xz, attended, output, up_own, up_halves, quarters
+    )
+    sums = product_sums(core, attended, output)
+    sums, up_own, up_halves, quarters, down_zh = together(sums, up_own, up_halves, quarters, down_zh)
+    sums = collect(sums)
+    up_zh = [swap(up_halves[0], ZH)]
+    up_x = swap(up_own, X)
+    down_zh.append(swap(quarters[3], ZH))
+    down_xz += [swap(down_zh[1], X), swap(down_zh[2], X)]
+    sums, up_zh, up_x, up_halves, down_zh, down_xz, all_cotangent = together(
+        sums, up_zh, up_x, up_halves, down_zh, down_xz, all_cotangent
+    )
+    middle, normal_two = middle_rows(sums, inputs, gains[1:])
+    normal_two = gather(normal_two, CORE, ZL, Y)
+    up_zh.append(swap(up_halves[1], ZH))
+    up_xz = [swap(up_zh[0], X)]
+    down_xz.append(swap(down_zh[3], X))
+    normal_two, up_zh, up_xz, down_xz = together(normal_two, up_zh, up_xz, down_xz)
+    up_xz.append(swap(up_zh[1], X))
+    down = place_rows(
+        places_of(
+            [(0, 0, down_places(0, 1, 2, 3))]
+            + [(0, 1, down_places(q)) for q in range(4)]
+            + [(1, 0, down_places(0, 1, 2, 3))]
+            + [(1, 1, down_places(q)) for q in range(4)]
+        ),
+        [down_weight, *down_zh, down_x, *down_xz],
+        half_block,
+    )
+    grad_activation = dot_transposed(all_cotangent, down)
+    activation, grad_hidden, up = feed_forward(
+        normal_two,
+        grad_activation,
+        places_of(
+            [(0, 0, column_places(0, 1)), (0, 1, column_places(0)), (0, 1, column_places(1))]
+            + [(1, 0, column_places(0, 1)), (1, 1, column_places(0)), (1, 1, column_places(1))]
+        ),
+        [up_own, *up_zh, up_x, *up_xz],
+        block,
+    )
+
+    def columns(left, right, start, stop, shape):
+        return contract_rows(left, right[:, start:stop]).astype(BF16).reshape(*shape, -1, stop - start)
+
+    cut = width * 3 // 4
+    partial = product_sums(core, grad_hidden, up, True)
+    down_most = columns(activation, all_cotangent, 0, cut, (2, 1, 2))
+    partial, activation, grad_hidden, down_most = together(partial, activation, grad_hidden, down_most)
+    sums = collect(partial)
+    down_rest = columns(activation, all_cotangent, cut, width, (2, 1, 2)).swapaxes(0, 2)
+    down_most_came = give(x, X, down_most)
+    down_rest_came = give(zh, ZH, down_rest)
+    middle_hidden = grad_hidden.shape[1] // 2
+    up_first = columns(normal_two, grad_hidden, 0, middle_hidden, (2, 2, 2))
+    sums, down_most_came, down_rest_came, up_first = together(sums, down_most_came, down_rest_came, up_first)
+    grad_middle, grad_branch = grad_middle_rows(sums, middle, cotangent, gains[1:])
+    grad_branch = gather(grad_branch, CORE, ZL, Y)
+    up_first_came = give(x, X, up_first)
+    down_rest_far = give_sum(zh, x, X, down_rest, down_rest_came)
+    down_most_far = give_sum(x, zh, ZH, down_most, down_most_came)
+    up_last = columns(normal_two, grad_hidden, middle_hidden, 2 * middle_hidden, (2, 2, 2))
+    output_partial = jnp.dot(activation, down, preferred_element_type=F32).astype(BF16)
+    grad_branch, down_rest_far, down_most_far, up_first_came, up_last, output_partial = together(
+        grad_branch, down_rest_far, down_most_far, up_first_came, up_last, output_partial
+    )
+    output_sums = lax.psum_scatter(
+        output_partial, AXES, scatter_dimension=0, tiled=True, axis_index_groups=alike(CORE, ZL, Y)
+    )
+    up_last_came = give(x, X, up_last)
+    up_first_far = give_sum(x, zh, ZH, up_first, up_first_came)
+    grad_attended = dot_transposed(grad_branch, output).astype(BF16)
+    grad_mixed = attention_backward_heads(ends, queries, keys, values, grad_attended, cosine, sine)
+    output_term = contract_rows(attended, grad_branch).astype(BF16)
+    output_term = output_term.reshape(2, 2, -1, width).swapaxes(0, 1)[:, None]
+    triple_term = columns(normal, grad_mixed, 0, grad_mixed.shape[1], (2, 2, 2))
+    grad_mixed, up_last_came, up_first_far, output_term, triple_term = together(
+        grad_mixed, up_last_came, up_first_far, output_term, triple_term
+    )
+    partial = product_sums(core, grad_mixed, triple, True)
+    triple_sent = lax.dynamic_index_in_dim(triple_term, 1 - x, 0, False)
+    partial, triple_sent, up_last_came = together(partial, triple_sent, up_last_came)
+    sums = collect(partial)
+    triple_came = swap(triple_sent, X)
+    up_last_far = give_sum(x, zh, ZH, up_last, up_last_came)
+    sums, triple_came, up_last_far, output_term, up_first_far = together(
+        sums, triple_came, up_last_far, output_term, up_first_far
+    )
+    triple_far = give_sum(x, zh, ZH, triple_term, triple_came)
+    output_came = give(x, X, output_term)
+    up_parts = [
+        keep_sum(x, zh, up_first, up_first_came, up_first_far),
+        keep_sum(x, zh, up_last, up_last_came, up_last_far),
+    ]
+    up_parts = [part.astype(BF16).reshape(MEMBERS, -1, middle_hidden) for part in up_parts]
+    up_slabs = exchange(jnp.concatenate(up_parts, axis=2), CORE, ZL, Y)
+    token_grad = token_grad_rows(sums, inputs, grad_middle, gains[:1])
+    triple_far, output_came, output_sums, token_grad, up_slabs = together(
+        triple_far, output_came, output_sums, token_grad, up_slabs
+    )
+    triple_sum = keep_sum(x, zh, triple_term, triple_came, triple_far).astype(BF16)
+    triple_sum = triple_sum.reshape(MEMBERS, -1, triple_sum.shape[-1])
+    triple_slabs = exchange(triple_sum, CORE, ZL, Y)
+    token_grad = regroup(token_grad)
+    layer_output = regroup((middle + output_sums.astype(F32)).astype(BF16))
+    output_far = give_sum(x, zh, ZH, output_term, output_came)
+    output_sum = keep_sum(x, zh, output_term, output_came, output_far)[0]
+    output_grad = lax.ppermute(output_sum.astype(BF16), AXES, turn_pairs()).astype(F32)
+    down_grad = jnp.concatenate(
+        [
+            keep_sum(x, zh, down_most, down_most_came, down_most_far)[0],
+            keep_sum(zh, x, down_rest, down_rest_came, down_rest_far)[0],
+        ],
+        axis=1,
+    )
+    triple_grad, first_gain_grad = place_columns(triple_slabs, triple_weight, first_column, triple_columns)
+    up_grad, second_gain_grad = place_columns(up_slabs, up_weight, second_column, up_columns)
+    return (
+        layer_output,
+        token_grad,
+        triple_grad,
+        output_grad,
+        up_grad,
+        down_grad,
+        first_gain_grad[:, 0],
+        second_gain_grad[:, 0],
+    )
+
+
 def solution(mesh):
+    grouped = mesh.shape["dp"] * 2 == mesh.shape["fsdp"] == MEMBERS
+    rows = P(AXES, None)
     return jax.shard_map(
-        body,
+        grouped_body if grouped else whole_rows_body,
         mesh=mesh,
-        in_specs=(
-            P(("dp", "fsdp"), None),
-            P(("dp", "fsdp"), None),
-            P(("dp", "fsdp"), None),
-            P(("dp", "fsdp"), None),
-            P(("dp", "fsdp"), None),
-            P(("dp", "fsdp")),
-            P(("dp", "fsdp")),
-            P(("dp", "fsdp"), None),
-            P("dp", None),
-            P("dp", None, None),
-            P("dp", None, None),
-        ),
-        out_specs=(
-            P(("dp", "fsdp"), None),
-            P(("dp", "fsdp"), None),
-            P(("dp", "fsdp"), None),
-            P(("dp", "fsdp"), None),
-            P(("dp", "fsdp"), None),
-            P(("dp", "fsdp"), None),
-            P(("dp", "fsdp")),
-            P(("dp", "fsdp")),
-        ),
+        in_specs=(rows,) * 5 + (P(AXES),) * 2 + (rows, P("dp", None), P("dp", None, None), P("dp", None, None)),
+        out_specs=(rows,) * 6 + (P(AXES),) * 2,
         check_vma=False,
     )

time: 4580 us -> 614 us (0.13)
  waiting for transfers between devices: 4060 us -> 283 us
  matrix products: 244 us -> 43.3 us
  blocking collectives: 193 us -> 0 us
  starting transfers between devices: 1.1 us -> 102 us
  Pallas kernels: 0 us -> 86.9 us
    reduce_scatter x4 -> x1, waiting for transfers between devices: 3390 us -> 0.01 us  [grouped_body(): lax.psum_scatter(output_partial, AXES, scatter_dimension=0, tiled=True, a...]
    all_gather x8 -> x4, waiting for transfers between devices: 676 us -> 25.2 us  [gather(): lax.all_gather(own, AXES, axis=0, tiled=True, axis_index_groups=alike(*bi...]
    ppermute x0 -> x43, waiting for transfers between devices: none -> 239 us  [the longest x37 216 us: swap(): return lax.ppermute(array, AXES, [(i, i ^ bits) for i in range(DEVICES)])]
    dot_general x19 -> x9, matrix products: 244 us -> 43.3 us  [the longest x6 25.5 us: contract_rows(): lax.dot_general(left, right, (((0,), (0,)), ((), ())), preferred_element_...]
    unnamed x2 -> x0, blocking collectives: 109 us -> none
    pallas_call x0 -> x18, Pallas kernels: none -> 86.9 us  [the longest x6 16.6 us: row_product(): pl.pallas_call(kernel, grid_spec=pltpu.PrefetchScalarGridSpec(num_scalar_...]
    all_gather x3 -> x0, blocking collectives: 84.7 us -> none  [the longest x1 32 us: body(): lax.all_gather(delta_rows.T, 'fsdp', axis=0, tiled=True)]
    ppermute x0 -> x43, starting transfers between devices: none -> 65 us  [the longest x37 49 us: swap(): return lax.ppermute(array, AXES, [(i, i ^ bits) for i in range(DEVICES)])]
  transfers between devices with their start and end apart: 12 -> 55, of which waited for: 10 -> 29; matrix products, arithmetic and copies ran while one was open for 6% -> 14% of each run, Pallas kernels for 0% -> 10%
where the time goes in v2:
time: 614 us; the launch traced here: 605 us
  waiting for transfers between devices  283 us (46%)
  starting transfers between devices  102 us (17%)
  Pallas kernels  86.9 us (14%)
  matrix products  43.3 us (7%)
  other arithmetic  39.4 us (6%)
  local copies, waits for them, and re-layouts  33.8 us (6%)
  between operations  16.3 us (3%)
    ppermute x37, waiting for transfers between devices, swap(): return lax.ppermute(array, AXES, [(i, i ^ bits) for i in range(DEVICES)])  216 us
    ppermute x37, starting transfers between devices, swap(): return lax.ppermute(array, AXES, [(i, i ^ bits) for i in range(DEVICES)])  49 us
    all_to_all x7, starting transfers between devices, exchange(): lax.all_to_all(array, AXES, 0, 0, tiled=True, axis_index_groups=alike(*bi...  36.3 us
    dot_general x6, matrix products, contract_rows(): lax.dot_general(left, right, (((0,), (0,)), ((), ())), preferred_element_...  25.5 us
    all_gather x4, waiting for transfers between devices, gather(): lax.all_gather(own, AXES, axis=0, tiled=True, axis_index_groups=alike(*bi...  25.2 us
    ppermute x4, waiting for transfers between devices, regroup(): return lax.ppermute(array, AXES, regroup_pairs())  23 us
    unnamed x117, local copies, waits for them, and re-layouts  19.1 us
    all_to_all x7, waiting for transfers between devices, exchange(): lax.all_to_all(array, AXES, 0, 0, tiled=True, axis_index_groups=alike(*bi...  18.4 us
  transfers between devices with their start and end apart: 55, of which 29 were waited for; matrix products, arithmetic and copies ran while one was open for 14% of the time, Pallas kernels for 10%

profile of v2, /device:TPU:1, one launch (start us, length us, event | category | flops | bytes accessed | tf_op | source)
XLA Modules:
  0.0 604.7 jit_solution(18380051866465516608)
XLA Ops:
  10.8 5.3 all-to-all-start
  17.7 4.8 collective-permute-start
  32.1 5.1 all-to-all-done
  39.4 7.1 %collective-permute-done.3.cotangent_ref = bf16[128,2048]{1,0:T(8,128)(2,1)} collective-permute-done((bf16[128,2048]{1,0:T(8,128)(2,1)}, bf16[128,2048]{1,0:T(8,128)(2,1)}, u32[]{:S(2)}, u32[]{:S(2)}) %collective-permute-start.3) | collective-permute-done | bytes 524320 | tf_op jit(solution)/shard_map/ppermute | solution.py:457
  46.7 5.1 collective-permute-start.6
  55.0 26.7 %collective-permute-done.7 = bf16[8,128]{1,0:T(8,128)(2,1)S(1)} collective-permute-done((bf16[8,128]{1,0:T(8,128)(2,1)S(1)}, bf16[8,128]{1,0:T(8,128)(2,1)S(1)}, u32[]{:S(2)}, u32[]{:S(2)}) %collective-permute-start.7) | collective-permute-done | bytes 2080 | tf_op jit(solution)/shard_map/ppermute | solution.py:426
  81.8 4.3 collective-permute-start.8
  87.8 5.0 all-gather.5.cloned.1.call-done.values_ref
  98.3 12.0 %shard_map.172.normal_ref = bf16[1024,2048]{1,0:T(8,128)(2,1)} custom-call(bf16[1024,2048]{1,0:T(8,128)(2,1)} %all-gather.5.cloned.1.call-done.values_ref, f32[1,2048]{1,0:T(1,128)} %get-tuple-element.253.gain_ref), custom_call_target="tpu_custom_call" | custom-call | tf_op jit(solution)/shard_map/pallas_call | solution.py:776
  110.3 4.7 collective-permute-done.10
  116.9 3.7 collective-permute-done.11.rest_1_
  121.5 4.8 all-to-all-start.1
  132.2 15.8 %shard_map.173 = (bf16[1024,256]{1,0:T(8,128)(2,1)S(1)}, bf16[1024,256]{1,0:T(8,128)(2,1)S(1)}, bf16[1024,256]{1,0:T(8,128)(2,1)S(1)}, bf16[1024,256]{1,0:T(8,128)(2,1)S(1)}, bf16[2048,768]{1,0:T(8,128)(2,1)}) custom-call(s32[2]{0:T(128)S(1)} %pad_add_fusion.1.ends_ref, s32[8]{0:T(128)S(1)} %stack.180.places_ref, bf16[1024,2048]{1,0:T(8,128)(2,1)} %shard_map.172.normal_ref, ...), custom_call_target="tpu_custom_call" | custom-call | tf_op jit(solution)/shard_map/pallas_call | solution.py:695
  150.3 11.4 %all-to-all-done.1 = bf16[8,64,1024]{2,1,0:T(8,128)(2,1)S(1)} async-done(((bf16[8,64,1024]{2,1,0:T(8,128)(2,1)}), bf16[8,64,1024]{2,1,0:T(8,128)(2,1)S(1)}, u32[]{:S(2)}, u32[]{:S(2)}) %all-to-all-start.1) | async-done | bytes 1048608 | tf_op jit(solution)/shard_map/all_to_all | solution.py:437
  165.1 3.8 collective-permute-done.16.rest_0_
  171.8 4.4 all-to-all-start.2
  181.2 34.8 %collective-permute-done.19.rest_4_ = bf16[64,2048]{1,0:T(8,128)(2,1)} collective-permute-done((bf16[64,2048]{1,0:T(8,128)(2,1)}, bf16[64,2048]{1,0:T(8,128)(2,1)}, u32[]{:S(2)}, u32[]{:S(2)}) %collective-permute-start.19) | collective-permute-done | bytes 262176 | tf_op jit(solution)/shard_map/ppermute | solution.py:426
  226.1 16.7 %collective-permute-done.24.rest_9_ = bf16[64,2048]{1,0:T(8,128)(2,1)} collective-permute-done((bf16[64,2048]{1,0:T(8,128)(2,1)}, bf16[64,2048]{1,0:T(8,128)(2,1)}, u32[]{:S(2)}, u32[]{:S(2)}) %collective-permute-start.24) | collective-permute-done | bytes 262176 | tf_op jit(solution)/shard_map/ppermute | solution.py:426
  242.8 4.8 collective-permute-done.22.rest_2_
  247.5 12.9 %all-gather.9.cloned.1.call-done.normal_ref = bf16[1024,2048]{1,0:T(8,128)(2,1)} async-done(((bf16[128,2048]{1,0:T(8,128)(2,1)}), bf16[1024,2048]{1,0:T(8,128)(2,1)}) %all-gather.9.cloned.1.call-update) | async-done | bytes 4194320 | tf_op jit(solution)/shard_map/all_gather | solution.py:465
  267.8 6.1 %fusion.29.grad_activation_ref = f32[1024,1024]{1,0:T(8,128)} fusion(bf16[1024,2048]{1,0:T(8,128)(2,1)S(1)} %copy-done.50, bf16[1024,2048]{1,0:T(8,128)(2,1)S(1)} %shard_map.177), kind=kOutput, calls=%fused_computation.85 | convolution fusion | flops 4294967296 | bytes 12582912 | tf_op jit(solution)/shard_map/dot_general | solution.py:888
  274.3 11.7 %shard_map.178 = (bf16[1024,1024]{1,0:T(8,128)(2,1)}, bf16[1024,1024]{1,0:T(8,128)(2,1)}, bf16[2048,1024]{1,0:T(8,128)(2,1)}) custom-call(s32[8]{0:T(128)S(1)} %stack.180.places_ref, bf16[1024,2048]{1,0:T(8,128)(2,1)} %all-gather.9.cloned.1.call-done.normal_ref, f32[1024,1024]{1,0:T(8,128)} %fusion.29.grad_activation_ref, bf16[512,1024]{1,0:T(8,128)(2,1)S(1)} %bitcast.182, ...), custom_call_target="tpu_custom_call" | custom-call | tf_op jit(solution)/shard_map/pallas_call | solution.py:867
  293.8 5.1 convolution_convert_fusion
  298.9 4.1 shard_map.180
  303.0 4.5 all-to-all-start.3
  319.3 3.8 convolution_convert_fusion.4
  323.1 18.7 %collective-permute-done.28 = bf16[1,2,256,512]{3,2,1,0:T(8,128)(2,1)} collective-permute-done((bf16[1,2,256,512]{3,2,1,0:T(8,128)(2,1)S(1)}, bf16[1,2,256,512]{3,2,1,0:T(8,128)(2,1)}, u32[]{:S(2)}, u32[]{:S(2)}) %collective-permute-start.28) | collective-permute-done | bytes 524320 | tf_op jit(solution)/shard_map/ppermute | solution.py:426
  341.8 4.8 collective-permute-done.27
  346.5 3.4 shard_map.181
  359.3 8.1 %convolution_convert_fusion.1 = bf16[1024,2048]{1,0:T(8,128)(2,1)} fusion(bf16[1024,1024]{1,0:T(8,128)(2,1)} %get-tuple-element.209, bf16[1024,2048]{1,0:T(8,128)(2,1)S(1)} %copy-done.11), kind=kOutput, calls=%fused_computation.1 | convolution fusion | flops 4297064448 | bytes 10485760 | tf_op jit(solution)/shard_map/dot_general | solution.py:1057
  368.9 5.9 convolution_convert_fusion.3
  374.8 12.7 %collective-permute-done.29 = bf16[1,256,512]{2,1,0:T(8,128)(2,1)S(1)} collective-permute-done((bf16[1,256,512]{2,1,0:T(8,128)(2,1)S(1)}, bf16[1,256,512]{2,1,0:T(8,128)(2,1)S(1)}, u32[]{:S(2)}, u32[]{:S(2)}) %collective-permute-start.29) | collective-permute-done | bytes 262176 | tf_op jit(solution)/shard_map/ppermute | solution.py:426
  389.9 7.3 %all-gather.11.cloned.1.call-done = bf16[1024,2048]{1,0:T(8,128)(2,1)} async-done(((bf16[128,2048]{1,0:T(8,128)(2,1)}), bf16[1024,2048]{1,0:T(8,128)(2,1)}) %all-gather.11.cloned.1.call-update) | async-done | bytes 4194320 | tf_op jit(solution)/shard_map/all_gather | solution.py:465
  397.2 3.6 convolution_convert_fusion.5
  407.5 3.6 convolution_convert_fusion.7.g_ref
  411.2 11.5 %shard_map.182.left_ref = bf16[1024,768]{1,0:T(8,128)(2,1)S(1)} custom-call(s32[2]{0:T(128)S(1)} %pad_add_fusion.1.ends_ref, bf16[1024,256]{1,0:T(8,128)(2,1)S(1)} %copy-done.23, bf16[1024,256]{1,0:T(8,128)(2,1)S(1)} %copy-done.25, bf16[1024,256]{1,0:T(8,128)(2,1)S(1)} %copy-done.27, bf16[1024,256]{1,0:T(8,128)(2,1)S(1)} %convolution_convert_fusion.7.g_ref, ...), custom_call_target="tpu_custom_call" | custom-call | tf_op jit(solution)/shard_map/pallas_call | solution.py:743
  422.8 3.8 convolution_convert_fusion.2
  438.8 3.6 shard_map.184
  442.4 5.8 all-to-all-start.4
  450.7 42.5 %collective-permute-done.36 = bf16[2,256,512]{2,1,0:T(8,128)(2,1)S(1)} collective-permute-done((bf16[2,256,512]{2,1,0:T(8,128)(2,1)S(1)}, bf16[2,256,512]{2,1,0:T(8,128)(2,1)S(1)}, u32[]{:S(2)}, u32[]{:S(2)}) %collective-permute-start.36) | collective-permute-done | bytes 524320 | tf_op jit(solution)/shard_map/ppermute | solution.py:426
  500.6 7.0 %all-to-all-start.5 = ((bf16[8,64,1024]{2,1,0:T(8,128)(2,1)}), bf16[8,64,1024]{2,1,0:T(8,128)(2,1)S(1)}, u32[]{:S(2)}, u32[]{:S(2)}) async-start(bf16[8,64,1024]{2,1,0:T(8,128)(2,1)} %pad_maximum_fusion.1), calls=%async_computation.6 | async-start | bytes 2097152 | tf_op jit(solution)/shard_map/all_to_all | solution.py:437
  519.9 6.3 %collective-permute-done.38 = bf16[1,2,64,2048]{3,2,1,0:T(8,128)(2,1)S(1)} collective-permute-done((bf16[1,2,64,2048]{3,2,1,0:T(8,128)(2,1)}, bf16[1,2,64,2048]{3,2,1,0:T(8,128)(2,1)S(1)}, u32[]{:S(2)}, u32[]{:S(2)}) %collective-permute-start.38) | collective-permute-done | bytes 524320 | tf_op jit(solution)/shard_map/ppermute | solution.py:426
  526.2 21.3 %collective-permute-done.37 = bf16[2,256,768]{2,1,0:T(8,128)(2,1)S(1)} collective-permute-done((bf16[2,256,768]{2,1,0:T(8,128)(2,1)}, bf16[2,256,768]{2,1,0:T(8,128)(2,1)S(1)}, u32[]{:S(2)}, u32[]{:S(2)}) %collective-permute-start.37) | collective-permute-done | bytes 786464 | tf_op jit(solution)/shard_map/ppermute | solution.py:426
  550.1 4.4 all-to-all-start.6
  558.4 4.1 collective-permute-start.39
  564.8 4.3 collective-permute-done.41
  577.2 10.1 %collective-permute-done.39 = bf16[128,2048]{1,0:T(8,128)(2,1)S(1)} collective-permute-done((bf16[128,2048]{1,0:T(8,128)(2,1)}, bf16[128,2048]{1,0:T(8,128)(2,1)S(1)}, u32[]{:S(2)}, u32[]{:S(2)}) %collective-permute-start.39) | collective-permute-done | bytes 524320 | tf_op jit(solution)/shard_map/ppermute | solution.py:457
  587.3 5.7 collective-permute-done.40
  (274 shorter events, 161.1 us)
Async XLA Ops:
  10.8 26.4 %all-to-all-start = ((bf16[8,80,768]{2,1,0:T(8,128)(2,1)}), bf16[8,80,768]{2,1,0:T(8,128)(2,1)S(1)}, u32[]{:S(2)}, u32[]{:S(2)}) async-start(bf16[8,80,768]{2,1,0:T(8,128)(2,1)} %shard_map.170), calls=%async_computation | async-start | bytes 1966080 | tf_op jit(solution)/shard_map/all_to_all | solution.py:437
  16.1 76.6 %all-gather.5.cloned.1.call-start = ((), (), s32[]{:S(2)}) async-start(), calls=%async_computation.8 | async-start | bytes 4718592 | tf_op jit(solution)/shard_map/all_gather | solution.py:465
  16.4 30.1 %collective-permute-start.1 = (bf16[256,2048]{1,0:T(8,128)(2,1)S(1)}, bf16[256,2048]{1,0:T(8,128)(2,1)S(1)}, u32[]{:S(2)}, u32[]{:S(2)}) collective-permute-start(bf16[256,2048]{1,0:T(8,128)(2,1)S(1)} %copy-done.9), channel_id=1, source_target_pairs={{0,16},{1,17},{2,18},{3,19},{4,20},{5,21},{6,22},{7,23},{8,24},{9,... | collective-permute-start | bytes 3145736 | tf_op jit(solution)/shard_map/ppermute | solution.py:426
  17.7 21.7 %collective-permute-start = (bf16[128,2048]{1,0:T(8,128)(2,1)}, bf16[128,2048]{1,0:T(8,128)(2,1)}, u32[]{:S(2)}, u32[]{:S(2)}) collective-permute-start(bf16[128,2048]{1,0:T(8,128)(2,1)} %param.11), channel_id=1, source_target_pairs={{0,0},{1,1},{2,2},{3,3},{4,8},{5,9},{6,10},{7,11},{8,4},{9,5},{10,... | collective-permute-start | bytes 1572872 | tf_op jit(solution)/shard_map/ppermute | solution.py:457
  22.5 24.1 %collective-permute-start.3 = (bf16[128,2048]{1,0:T(8,128)(2,1)}, bf16[128,2048]{1,0:T(8,128)(2,1)}, u32[]{:S(2)}, u32[]{:S(2)}) collective-permute-start(bf16[128,2048]{1,0:T(8,128)(2,1)} %param.18), channel_id=1, source_target_pairs={{0,0},{1,1},{2,2},{3,3},{4,8},{5,9},{6,10},{7,11},{8,4},{9,5},{10,... | collective-permute-start | bytes 1572872 | tf_op jit(solution)/shard_map/ppermute | solution.py:457
  24.4 15.0 %collective-permute-start.2 = (bf16[64,2048]{1,0:T(8,128)(2,1)S(1)}, bf16[64,2048]{1,0:T(8,128)(2,1)}, u32[]{:S(2)}, u32[]{:S(2)}) collective-permute-start(bf16[64,2048]{1,0:T(8,128)(2,1)S(1)} %copy-done.52), channel_id=1, source_target_pairs={{0,0},{1,16},{2,2},{3,18},{4,4},{5,20},{6,6},{7,22},{8,8},{9,24},{... | collective-permute-start | bytes 786440 | tf_op jit(solution)/shard_map/ppermute | solution.py:952
  46.6 41.1 %collective-permute-start.5 = (bf16[512,768]{1,0:T(8,128)(2,1)S(1)}, bf16[512,768]{1,0:T(8,128)(2,1)}, u32[]{:S(2)}, u32[]{:S(2)}) collective-permute-start(bf16[512,768]{1,0:T(8,128)(2,1)S(1)} %bitcast.187), channel_id=1, source_target_pairs={{0,4},{1,5},{2,6},{3,7},{4,0},{5,1},{6,2},{7,3},{8,12},{9,13},{10,... | collective-permute-start | bytes 2359304 | tf_op jit(solution)/shard_map/ppermute | solution.py:426
  46.7 41.1 %collective-permute-start.6 = (bf16[512,768]{1,0:T(8,128)(2,1)S(1)}, bf16[512,768]{1,0:T(8,128)(2,1)}, u32[]{:S(2)}, u32[]{:S(2)}) collective-permute-start(bf16[512,768]{1,0:T(8,128)(2,1)S(1)} %bitcast.188), channel_id=1, source_target_pairs={{0,16},{1,17},{2,18},{3,19},{4,20},{5,21},{6,22},{7,23},{8,24},{9,... | collective-permute-start | bytes 2359304 | tf_op jit(solution)/shard_map/ppermute | solution.py:426
  54.4 27.3 %collective-permute-start.7 = (bf16[8,128]{1,0:T(8,128)(2,1)S(1)}, bf16[8,128]{1,0:T(8,128)(2,1)S(1)}, u32[]{:S(2)}, u32[]{:S(2)}) collective-permute-start(bf16[8,128]{1,0:T(8,128)(2,1)S(1)} %bitcast.215), channel_id=1, source_target_pairs={{0,4},{1,5},{2,6},{3,7},{4,0},{5,1},{6,2},{7,3},{8,12},{9,13},{10,... | collective-permute-start | bytes 6152 | tf_op jit(solution)/shard_map/ppermute | solution.py:426
  92.7 27.9 %collective-permute-start.9 = (bf16[512,768]{1,0:T(8,128)(2,1)}, bf16[512,768]{1,0:T(8,128)(2,1)S(1)}, u32[]{:S(2)}, u32[]{:S(2)}) collective-permute-start(bf16[512,768]{1,0:T(8,128)(2,1)} %collective-permute-done.5.rest_1_), channel_id=1, source_target_pairs={{0,16},{1,17},{2,18},{3,19},{4,20},{5,21},{6,22},{7,23},{8,24},{9,... | collective-permute-start | bytes 2359304 | tf_op jit(solution)/shard_map/ppermute | solution.py:426
  95.3 19.7 %collective-permute-start.10 = (bf16[64,2048]{1,0:T(8,128)(2,1)}, bf16[64,2048]{1,0:T(8,128)(2,1)S(1)}, u32[]{:S(2)}, u32[]{:S(2)}) collective-permute-start(bf16[64,2048]{1,0:T(8,128)(2,1)} %collective-permute-done.2), channel_id=1, source_target_pairs={{0,4},{1,5},{2,6},{3,7},{4,0},{5,1},{6,2},{7,3},{8,12},{9,13},{10,... | collective-permute-start | bytes 786440 | tf_op jit(solution)/shard_map/ppermute | solution.py:426
  95.3 25.3 %collective-permute-start.11 = (bf16[64,2048]{1,0:T(8,128)(2,1)}, bf16[64,2048]{1,0:T(8,128)(2,1)S(1)}, u32[]{:S(2)}, u32[]{:S(2)}) collective-permute-start(bf16[64,2048]{1,0:T(8,128)(2,1)} %get-tuple-element.141), channel_id=1, source_target_pairs={{0,4},{1,5},{2,6},{3,7},{4,0},{5,1},{6,2},{7,3},{8,12},{9,13},{10,... | collective-permute-start | bytes 786440 | tf_op jit(solution)/shard_map/ppermute | solution.py:426
  121.5 40.2 %all-to-all-start.1 = ((bf16[8,64,1024]{2,1,0:T(8,128)(2,1)}), bf16[8,64,1024]{2,1,0:T(8,128)(2,1)S(1)}, u32[]{:S(2)}, u32[]{:S(2)}) async-start(bf16[8,64,1024]{2,1,0:T(8,128)(2,1)} %shard_map.171), calls=%async_computation.1 | async-start | bytes 2097152 | tf_op jit(solution)/shard_map/all_to_all | solution.py:437
  126.4 92.1 %all-gather.7.cloned.1.call-start = ((), (), s32[]{:S(2)}) async-start(), calls=%async_computation.9 | async-start | bytes 4718592 | tf_op jit(solution)/shard_map/all_gather | solution.py:465
  127.1 21.0 %collective-permute-start.15 = (bf16[2,64,2048]{2,1,0:T(8,128)(2,1)}, bf16[2,64,2048]{2,1,0:T(8,128)(2,1)}, u32[]{:S(2)}, u32[]{:S(2)}) collective-permute-start(bf16[2,64,2048]{2,1,0:T(8,128)(2,1)} %maximum_select_fusion.1), channel_id=1, source_target_pairs={{0,16},{1,17},{2,18},{3,19},{4,20},{5,21},{6,22},{7,23},{8,24},{9,... | collective-permute-start | bytes 1572872 | tf_op jit(solution)/shard_map/ppermute | solution.py:426
  127.3 35.5 %collective-permute-start.12 = (bf16[64,2048]{1,0:T(8,128)(2,1)}, bf16[64,2048]{1,0:T(8,128)(2,1)}, u32[]{:S(2)}, u32[]{:S(2)}) collective-permute-start(bf16[64,2048]{1,0:T(8,128)(2,1)} %get-tuple-element.147), channel_id=1, source_target_pairs={{0,4},{1,5},{2,6},{3,7},{4,0},{5,1},{6,2},{7,3},{8,12},{9,13},{10,... | collective-permute-start | bytes 786440 | tf_op jit(solution)/shard_map/ppermute | solution.py:426
  128.3 34.5 %collective-permute-start.13 = (bf16[64,2048]{1,0:T(8,128)(2,1)}, bf16[64,2048]{1,0:T(8,128)(2,1)}, u32[]{:S(2)}, u32[]{:S(2)}) collective-permute-start(bf16[64,2048]{1,0:T(8,128)(2,1)} %get-tuple-element.148), channel_id=1, source_target_pairs={{0,4},{1,5},{2,6},{3,7},{4,0},{5,1},{6,2},{7,3},{8,12},{9,13},{10,... | collective-permute-start | bytes 786440 | tf_op jit(solution)/shard_map/ppermute | solution.py:426
  129.7 33.1 %collective-permute-start.14 = (bf16[64,2048]{1,0:T(8,128)(2,1)S(1)}, bf16[64,2048]{1,0:T(8,128)(2,1)}, u32[]{:S(2)}, u32[]{:S(2)}) collective-permute-start(bf16[64,2048]{1,0:T(8,128)(2,1)S(1)} %collective-permute-done.11.rest_1_), channel_id=1, source_target_pairs={{0,16},{1,17},{2,18},{3,19},{4,20},{5,21},{6,22},{7,23},{8,24},{9,... | collective-permute-start | bytes 786440 | tf_op jit(solution)/shard_map/ppermute | solution.py:426
  171.8 46.6 %all-to-all-start.2 = ((bf16[4,128,2048]{2,1,0:T(8,128)(2,1)}), bf16[4,128,2048]{2,1,0:T(8,128)(2,1)}, u32[]{:S(2)}, u32[]{:S(2)}) async-start(bf16[4,128,2048]{2,1,0:T(8,128)(2,1)} %bitcast.186), calls=%async_computation.2 | async-start | bytes 4194304 | tf_op jit(solution)/shard_map/all_to_all | solution.py:437
  176.3 84.2 %all-gather.9.cloned.1.call-start = ((), (), s32[]{:S(2)}) async-start(), calls=%async_computation.10 | async-start | bytes 4718592 | tf_op jit(solution)/shard_map/all_gather | solution.py:465
  176.5 41.0 %collective-permute-start.18 = (bf16[512,1024]{1,0:T(8,128)(2,1)S(1)}, bf16[512,1024]{1,0:T(8,128)(2,1)S(1)}, u32[]{:S(2)}, u32[]{:S(2)}) collective-permute-start(bf16[512,1024]{1,0:T(8,128)(2,1)S(1)} %bitcast.181), channel_id=1, source_target_pairs={{0,16},{1,17},{2,18},{3,19},{4,20},{5,21},{6,22},{7,23},{8,24},{9,... | collective-permute-start | bytes 3145736 | tf_op jit(solution)/shard_map/ppermute | solution.py:426
  176.6 40.9 %collective-permute-start.17 = (bf16[256,1024]{1,0:T(8,128)(2,1)}, bf16[256,1024]{1,0:T(8,128)(2,1)}, u32[]{:S(2)}, u32[]{:S(2)}) collective-permute-start(bf16[256,1024]{1,0:T(8,128)(2,1)} %bitcast.213), channel_id=1, source_target_pairs={{0,4},{1,5},{2,6},{3,7},{4,0},{5,1},{6,2},{7,3},{8,12},{9,13},{10,... | collective-permute-start | bytes 1572872 | tf_op jit(solution)/shard_map/ppermute | solution.py:426
  179.7 36.3 %collective-permute-start.19 = (bf16[64,2048]{1,0:T(8,128)(2,1)}, bf16[64,2048]{1,0:T(8,128)(2,1)}, u32[]{:S(2)}, u32[]{:S(2)}) collective-permute-start(bf16[64,2048]{1,0:T(8,128)(2,1)} %get-tuple-element.175), channel_id=1, source_target_pairs={{0,4},{1,5},{2,6},{3,7},{4,0},{5,1},{6,2},{7,3},{8,12},{9,13},{10,... | collective-permute-start | bytes 786440 | tf_op jit(solution)/shard_map/ppermute | solution.py:426
  179.8 36.3 %collective-permute-start.20 = (bf16[64,2048]{1,0:T(8,128)(2,1)}, bf16[64,2048]{1,0:T(8,128)(2,1)S(1)}, u32[]{:S(2)}, u32[]{:S(2)}) collective-permute-start(bf16[64,2048]{1,0:T(8,128)(2,1)} %collective-permute-done.12.rest_2_), channel_id=1, source_target_pairs={{0,16},{1,17},{2,18},{3,19},{4,20},{5,21},{6,22},{7,23},{8,24},{9,... | collective-permute-start | bytes 786440 | tf_op jit(solution)/shard_map/ppermute | solution.py:426
  181.1 35.7 %collective-permute-start.21 = (bf16[64,2048]{1,0:T(8,128)(2,1)}, bf16[64,2048]{1,0:T(8,128)(2,1)S(1)}, u32[]{:S(2)}, u32[]{:S(2)}) collective-permute-start(bf16[64,2048]{1,0:T(8,128)(2,1)} %collective-permute-done.13.rest_3_), channel_id=1, source_target_pairs={{0,16},{1,17},{2,18},{3,19},{4,20},{5,21},{6,22},{7,23},{8,24},{9,... | collective-permute-start | bytes 786440 | tf_op jit(solution)/shard_map/ppermute | solution.py:426
  221.3 26.2 %collective-permute-start.22 = (bf16[256,1024]{1,0:T(8,128)(2,1)}, bf16[256,1024]{1,0:T(8,128)(2,1)}, u32[]{:S(2)}, u32[]{:S(2)}) collective-permute-start(bf16[256,1024]{1,0:T(8,128)(2,1)} %bitcast.212), channel_id=1, source_target_pairs={{0,4},{1,5},{2,6},{3,7},{4,0},{5,1},{6,2},{7,3},{8,12},{9,13},{10,... | collective-permute-start | bytes 1572872 | tf_op jit(solution)/shard_map/ppermute | solution.py:426
  224.5 23.0 %collective-permute-start.23 = (bf16[256,1024]{1,0:T(8,128)(2,1)}, bf16[256,1024]{1,0:T(8,128)(2,1)}, u32[]{:S(2)}, u32[]{:S(2)}) collective-permute-start(bf16[256,1024]{1,0:T(8,128)(2,1)} %collective-permute-done.17.rest_1_), channel_id=1, source_target_pairs={{0,16},{1,17},{2,18},{3,19},{4,20},{5,21},{6,22},{7,23},{8,24},{9,... | collective-permute-start | bytes 1572872 | tf_op jit(solution)/shard_map/ppermute | solution.py:426
  224.5 18.3 %collective-permute-start.24 = (bf16[64,2048]{1,0:T(8,128)(2,1)}, bf16[64,2048]{1,0:T(8,128)(2,1)}, u32[]{:S(2)}, u32[]{:S(2)}) collective-permute-start(bf16[64,2048]{1,0:T(8,128)(2,1)} %collective-permute-done.19.rest_4_), channel_id=1, source_target_pairs={{0,16},{1,17},{2,18},{3,19},{4,20},{5,21},{6,22},{7,23},{8,24},{9,... | collective-permute-start | bytes 786440 | tf_op jit(solution)/shard_map/ppermute | solution.py:426
  260.5 13.8 %collective-permute-start.25 = (bf16[256,1024]{1,0:T(8,128)(2,1)}, bf16[256,1024]{1,0:T(8,128)(2,1)S(1)}, u32[]{:S(2)}, u32[]{:S(2)}) collective-permute-start(bf16[256,1024]{1,0:T(8,128)(2,1)} %collective-permute-done.22.rest_2_), channel_id=1, source_target_pairs={{0,16},{1,17},{2,18},{3,19},{4,20},{5,21},{6,22},{7,23},{8,24},{9,... | collective-permute-start | bytes 1572872 | tf_op jit(solution)/shard_map/ppermute | solution.py:426
  303.0 43.5 %all-to-all-start.3 = ((bf16[4,128,2048]{2,1,0:T(8,128)(2,1)}), bf16[4,128,2048]{2,1,0:T(8,128)(2,1)}, u32[]{:S(2)}, u32[]{:S(2)}) async-start(bf16[4,128,2048]{2,1,0:T(8,128)(2,1)} %bitcast.45), calls=%async_computation.3 | async-start | bytes 4194304 | tf_op jit(solution)/shard_map/all_to_all | solution.py:437
  307.5 89.7 %all-gather.11.cloned.1.call-start = ((), (), s32[]{:S(2)}) async-start(), calls=%async_computation.11 | async-start | bytes 4718592 | tf_op jit(solution)/shard_map/all_gather | solution.py:465
  310.2 36.3 %collective-permute-start.27 = (bf16[1,2,256,1536]{3,2,1,0:T(8,128)(2,1)}, bf16[1,2,256,1536]{3,2,1,0:T(8,128)(2,1)}, u32[]{:S(2)}, u32[]{:S(2)}) collective-permute-start(bf16[1,2,256,1536]{3,2,1,0:T(8,128)(2,1)} %dynamic-slice_bitcast_fusion), channel_id=1, source_target_pairs={{0,16},{1,17},{2,18},{3,19},{4,20},{5,21},{6,22},{7,23},{8,24},{9,... | collective-permute-start | bytes 4718600 | tf_op jit(solution)/shard_map/ppermute | solution.py:426
  316.0 25.8 %collective-permute-start.28 = (bf16[1,2,256,512]{3,2,1,0:T(8,128)(2,1)S(1)}, bf16[1,2,256,512]{3,2,1,0:T(8,128)(2,1)}, u32[]{:S(2)}, u32[]{:S(2)}) collective-permute-start(bf16[1,2,256,512]{3,2,1,0:T(8,128)(2,1)S(1)} %dynamic-slice_bitcast_fusion.2), channel_id=1, source_target_pairs={{0,4},{1,5},{2,6},{3,7},{4,0},{5,1},{6,2},{7,3},{8,12},{9,13},{10,... | collective-permute-start | bytes 1572872 | tf_op jit(solution)/shard_map/ppermute | solution.py:426
  350.0 197.6 %reduce-scatter.2.cloned.1.call-start = ((), (), s32[]{:S(2)}) async-start(), calls=%async_computation.12 | async-start | bytes 4718592 | tf_op jit(solution)/shard_map/reduce_scatter | solution.py:1061
  352.6 37.3 %collective-permute-start.30 = (bf16[1,256,1536]{2,1,0:T(8,128)(2,1)}, bf16[1,256,1536]{2,1,0:T(8,128)(2,1)}, u32[]{:S(2)}, u32[]{:S(2)}) collective-permute-start(bf16[1,256,1536]{2,1,0:T(8,128)(2,1)} %fusion.6), channel_id=1, source_target_pairs={{0,4},{1,5},{2,6},{3,7},{4,0},{5,1},{6,2},{7,3},{8,12},{9,13},{10,... | collective-permute-start | bytes 2359304 | tf_op jit(solution)/shard_map/ppermute | solution.py:426
  358.3 31.6 %collective-permute-start.31 = (bf16[2,2,256,512]{3,2,0,1:T(8,128)(2,1)}, bf16[2,2,256,512]{3,2,0,1:T(8,128)(2,1)}, u32[]{:S(2)}, u32[]{:S(2)}) collective-permute-start(bf16[2,2,256,512]{3,2,0,1:T(8,128)(2,1)} %copy_bitcast_fusion.3), channel_id=1, source_target_pairs={{0,16},{1,17},{2,18},{3,19},{4,20},{5,21},{6,22},{7,23},{8,24},{9,... | collective-permute-start | bytes 3145736 | tf_op jit(solution)/shard_map/ppermute | solution.py:426
  368.4 19.0 %collective-permute-start.29 = (bf16[1,256,512]{2,1,0:T(8,128)(2,1)S(1)}, bf16[1,256,512]{2,1,0:T(8,128)(2,1)S(1)}, u32[]{:S(2)}, u32[]{:S(2)}) collective-permute-start(bf16[1,256,512]{2,1,0:T(8,128)(2,1)S(1)} %fusion.21), channel_id=1, source_target_pairs={{0,16},{1,17},{2,18},{3,19},{4,20},{5,21},{6,22},{7,23},{8,24},{9,... | collective-permute-start | bytes 786440 | tf_op jit(solution)/shard_map/ppermute | solution.py:426
  404.1 25.7 %collective-permute-start.33 = (bf16[2,256,512]{2,1,0:T(8,128)(2,1)}, bf16[2,256,512]{2,1,0:T(8,128)(2,1)}, u32[]{:S(2)}, u32[]{:S(2)}) collective-permute-start(bf16[2,256,512]{2,1,0:T(8,128)(2,1)} %fusion.12), channel_id=1, source_target_pairs={{0,4},{1,5},{2,6},{3,7},{4,0},{5,1},{6,2},{7,3},{8,12},{9,13},{10,... | collective-permute-start | bytes 1572872 | tf_op jit(solution)/shard_map/ppermute | solution.py:426
  406.4 24.3 %collective-permute-start.32 = (bf16[2,2,256,512]{3,2,0,1:T(8,128)(2,1)}, bf16[2,2,256,512]{3,2,0,1:T(8,128)(2,1)S(1)}, u32[]{:S(2)}, u32[]{:S(2)}) collective-permute-start(bf16[2,2,256,512]{3,2,0,1:T(8,128)(2,1)} %copy_bitcast_fusion.2), channel_id=1, source_target_pairs={{0,16},{1,17},{2,18},{3,19},{4,20},{5,21},{6,22},{7,23},{8,24},{9,... | collective-permute-start | bytes 3145736 | tf_op jit(solution)/shard_map/ppermute | solution.py:426
  442.4 53.4 %all-to-all-start.4 = ((bf16[4,128,2048]{2,1,0:T(8,128)(2,1)}), bf16[4,128,2048]{2,1,0:T(8,128)(2,1)S(1)}, u32[]{:S(2)}, u32[]{:S(2)}) async-start(bf16[4,128,2048]{2,1,0:T(8,128)(2,1)} %bitcast.67), calls=%async_computation.4 | async-start | bytes 4194304 | tf_op jit(solution)/shard_map/all_to_all | solution.py:437
  448.2 45.8 %collective-permute-start.35 = (bf16[2,2,256,768]{3,2,0,1:T(8,128)(2,1)}, bf16[2,2,256,768]{3,2,0,1:T(8,128)(2,1)}, u32[]{:S(2)}, u32[]{:S(2)}) collective-permute-start(bf16[2,2,256,768]{3,2,0,1:T(8,128)(2,1)} %copy_bitcast_fusion), channel_id=1, source_target_pairs={{0,16},{1,17},{2,18},{3,19},{4,20},{5,21},{6,22},{7,23},{8,24},{9,... | collective-permute-start | bytes 4718600 | tf_op jit(solution)/shard_map/ppermute | solution.py:426
  450.6 42.6 %collective-permute-start.36 = (bf16[2,256,512]{2,1,0:T(8,128)(2,1)S(1)}, bf16[2,256,512]{2,1,0:T(8,128)(2,1)S(1)}, u32[]{:S(2)}, u32[]{:S(2)}) collective-permute-start(bf16[2,256,512]{2,1,0:T(8,128)(2,1)S(1)} %fusion.11), channel_id=1, source_target_pairs={{0,4},{1,5},{2,6},{3,7},{4,0},{5,1},{6,2},{7,3},{8,12},{9,13},{10,... | collective-permute-start | bytes 1572872 | tf_op jit(solution)/shard_map/ppermute | solution.py:426
  500.6 47.0 %all-to-all-start.5 = ((bf16[8,64,1024]{2,1,0:T(8,128)(2,1)}), bf16[8,64,1024]{2,1,0:T(8,128)(2,1)S(1)}, u32[]{:S(2)}, u32[]{:S(2)}) async-start(bf16[8,64,1024]{2,1,0:T(8,128)(2,1)} %pad_maximum_fusion.1), calls=%async_computation.6 | async-start | bytes 2097152 | tf_op jit(solution)/shard_map/all_to_all | solution.py:437
  510.4 37.2 %collective-permute-start.37 = (bf16[2,256,768]{2,1,0:T(8,128)(2,1)}, bf16[2,256,768]{2,1,0:T(8,128)(2,1)S(1)}, u32[]{:S(2)}, u32[]{:S(2)}) collective-permute-start(bf16[2,256,768]{2,1,0:T(8,128)(2,1)} %fusion.5), channel_id=1, source_target_pairs={{0,4},{1,5},{2,6},{3,7},{4,0},{5,1},{6,2},{7,3},{8,12},{9,13},{10,... | collective-permute-start | bytes 2359304 | tf_op jit(solution)/shard_map/ppermute | solution.py:426
  512.5 13.8 %collective-permute-start.38 = (bf16[1,2,64,2048]{3,2,1,0:T(8,128)(2,1)}, bf16[1,2,64,2048]{3,2,1,0:T(8,128)(2,1)S(1)}, u32[]{:S(2)}, u32[]{:S(2)}) collective-permute-start(bf16[1,2,64,2048]{3,2,1,0:T(8,128)(2,1)} %dynamic-slice_bitcast_fusion.1), channel_id=1, source_target_pairs={{0,16},{1,17},{2,18},{3,19},{4,20},{5,21},{6,22},{7,23},{8,24},{9,... | collective-permute-start | bytes 1572872 | tf_op jit(solution)/shard_map/ppermute | solution.py:426
  550.1 42.9 %all-to-all-start.6 = ((bf16[8,64,768]{2,1,0:T(8,128)(2,1)}), bf16[8,64,768]{2,1,0:T(8,128)(2,1)S(1)}, u32[]{:S(2)}, u32[]{:S(2)}) async-start(bf16[8,64,768]{2,1,0:T(8,128)(2,1)} %bitcast.80), calls=%async_computation.7 | async-start | bytes 1572864 | tf_op jit(solution)/shard_map/all_to_all | solution.py:437
  558.4 28.9 %collective-permute-start.39 = (bf16[128,2048]{1,0:T(8,128)(2,1)}, bf16[128,2048]{1,0:T(8,128)(2,1)S(1)}, u32[]{:S(2)}, u32[]{:S(2)}) collective-permute-start(bf16[128,2048]{1,0:T(8,128)(2,1)} %add_convert_fusion), channel_id=1, source_target_pairs={{0,0},{1,1},{2,2},{3,3},{4,8},{5,9},{6,10},{7,11},{8,4},{9,5},{10,... | collective-permute-start | bytes 1572872 | tf_op jit(solution)/shard_map/ppermute | solution.py:457
  562.5 30.5 %collective-permute-start.40 = (bf16[128,2048]{1,0:T(8,128)(2,1)}, bf16[128,2048]{1,0:T(8,128)(2,1)}, u32[]{:S(2)}, u32[]{:S(2)}) collective-permute-start(bf16[128,2048]{1,0:T(8,128)(2,1)} %shard_map.185), channel_id=1, source_target_pairs={{0,0},{1,1},{2,2},{3,3},{4,8},{5,9},{6,10},{7,11},{8,4},{9,5},{10,... | collective-permute-start | bytes 1572872 | tf_op jit(solution)/shard_map/ppermute | solution.py:457
  (64 other events, 530.0 us)
Sparse Core Ops, SparseCore 0:
  46.7 45.9 all-gather.4
  128.8 41.5 all-gather.6
  221.5 38.9 all-gather.8
  350.1 47.0 all-gather.10
  407.6 124.3 reduce-scatter.1
